TPU v7x, 256 devices: a whole 4x4x8 slice. The times are simulated.
256 devices in a mesh: group: 16 (over y, x_lo, core), fsdp: 16 (over x_hi, z).
Axes of the slice: x: 4 (x_hi: 2, x_lo: 2; x = x_hi * 2 + x_lo), y: 4, z: 8, core: 2. Of those that a mesh axis runs over, the one named last changes fastest.
Arguments:
- inputs: bfloat16 [16, 5120, 5120], P('group', 'fsdp'), may hold values from -6 to 6
- key_grad: bfloat16 [16, 5120, 1024], P('group', 'fsdp'), may hold values from -6 to 6
- seg_ids: int32 [16, 5120], P('group', 'fsdp'), may hold values from 0 to 15, never falling along the last dimension, each value on 1 to 2560 neighbouring positions
- advantages: float32 [16, 16], P('group'), may hold values from -4 to 4
- gains: bfloat16 [16, 5120], P('group', 'fsdp'), may hold values from 0.5 to 1.5
- local_weights: bfloat16 [16, 5120, 1024], P('group', 'fsdp'), may hold values from -6 to 6
- outer_weights: float32 [5120, 1024], P('fsdp'), may hold values from -6 to 6
- momentum: float32 [5120, 1024], P('fsdp'), may hold values from -3 to 3
- frag_index: int32 [1], replicated, may hold values from 0 to 3
Outputs:
- keys: bfloat16 [16, 5120, 1024], P('group', 'fsdp')
- input_grad: bfloat16 [16, 5120, 5120], P('group', 'fsdp')
- weight_grad: bfloat16 [16, 5120, 1024], P('group', 'fsdp')
- gain_grad: float32 [16, 5120], P('group', 'fsdp')
- new_outer: float32 [5120, 256], P('fsdp')
- new_momentum: float32 [5120, 256], P('fsdp')
Inputs may be any that keep to these rules, and one draw needn't show every extreme that they name: `seg_ids`: each of the 16 sequences of a group holds one or more tokens.
All inputs are finite; a program needn't handle non-finite values.
Results may differ from a plain program's by a relative error of at most 0.019.
Values may be sent and summed in bfloat16 or wider, within the bound.
A program may use at most 128 MiB of HBM per device.

v0:
```python
import jax
import jax.numpy as jnp
from jax import lax
from jax.sharding import PartitionSpec as P

NFRAG = 4


EPSILON = 1e-06
OUTER_MU = 0.9
OUTER_LR = 0.7


def outer_update(pseudo_grad, outer_frag, moment_frag):
    new_momentum = OUTER_MU * moment_frag + pseudo_grad
    new_outer = outer_frag - OUTER_LR * (pseudo_grad + OUTER_MU * new_momentum)
    return (new_outer, new_momentum)


def local(
    inputs, key_grad, seg_ids, advantages, gains, local_weights, outer_weights, momentum, frag_index
):
    tok_rows = inputs.shape[1]
    unit_scale = inputs.shape[2] ** (-0.5)
    float_in = inputs[0].astype(jnp.float32)
    inv_rms = lax.rsqrt(jnp.mean(float_in * float_in, -1, keepdims=True) + EPSILON)
    unit_rows = float_in * inv_rms
    gain_full, weight_full = (
        lax.all_gather(gains[0], "fsdp", axis=0, tiled=True),
        lax.all_gather(local_weights[0], "fsdp", axis=0, tiled=True),
    )
    gain_float = gain_full.astype(jnp.float32)
    normed = (unit_rows * gain_float).astype(jnp.bfloat16)
    keys = (jnp.dot(normed, weight_full, preferred_element_type=jnp.float32) * unit_scale).astype(
        jnp.bfloat16
    )
    seq_count = advantages.shape[1]
    onehot = seg_ids[0][:, None] == jnp.arange(seq_count, dtype=jnp.int32)[None, :]
    lengths = lax.psum(jnp.sum(onehot.astype(jnp.int32), 0), "fsdp")
    group_tokens = tok_rows * lax.axis_size("fsdp")
    floor_len = group_tokens / (2 * seq_count)
    per_seq = (
        advantages[0]
        * (group_tokens / seq_count)
        / jnp.maximum(lengths.astype(jnp.float32), floor_len)
    )
    token_weight = jnp.sum(jnp.where(onehot, per_seq[None, :], jnp.float32(0.0)), 1)
    cotangent = (key_grad[0].astype(jnp.float32) * token_weight[:, None]).astype(jnp.bfloat16)
    grad_norm = (
        lax.dot_general(
            cotangent,
            lax.all_gather(local_weights[0], "fsdp", axis=0, tiled=True),
            (((1,), (1,)), ((), ())),
            preferred_element_type=jnp.float32,
        )
        * unit_scale
    )
    scaled_grad = grad_norm * gain_float
    input_grad = (
        inv_rms * (scaled_grad - unit_rows * jnp.mean(scaled_grad * unit_rows, -1, keepdims=True))
    ).astype(jnp.bfloat16)
    weight_term = (
        lax.dot_general(
            normed, cotangent, (((0,), (0,)), ((), ())), preferred_element_type=jnp.float32
        )
        * unit_scale
    )
    gain_term = jnp.sum(grad_norm * unit_rows, 0)
    weight_grad, gain_grad = (
        lax.psum_scatter(
            weight_term.astype(jnp.bfloat16), "fsdp", scatter_dimension=0, tiled=True
        ).astype(jnp.float32),
        lax.psum_scatter(
            gain_term.astype(jnp.bfloat16), "fsdp", scatter_dimension=0, tiled=True
        ).astype(jnp.float32),
    )
    frag_cols = outer_weights.shape[1] // NFRAG
    fragment = frag_index[0] * frag_cols
    outer_frag = lax.dynamic_slice_in_dim(outer_weights, fragment, frag_cols, 1)
    moment_frag = lax.dynamic_slice_in_dim(momentum, fragment, frag_cols, 1)
    local_frag = lax.dynamic_slice_in_dim(local_weights[0], fragment, frag_cols, 1).astype(
        jnp.float32
    )
    pseudo_term = outer_frag - local_frag
    group_count = lax.axis_size("group")
    summed = lax.psum(pseudo_term, "group")
    new_outer, new_momentum = outer_update(summed / group_count, outer_frag, moment_frag)
    return (
        keys[None],
        input_grad[None],
        weight_grad.astype(jnp.bfloat16)[None],
        gain_grad[None],
        new_outer,
        new_momentum,
    )


def solution(mesh):
    in_specs = (
        P("group", "fsdp", None),
        P("group", "fsdp", None),
        P("group", "fsdp"),
        P("group", None),
        P("group", "fsdp"),
        P("group", "fsdp", None),
        P("fsdp", None),
        P("fsdp", None),
        P(),
    )
    out_specs = (
        P("group", "fsdp", None),
        P("group", "fsdp", None),
        P("group", "fsdp", None),
        P("group", "fsdp"),
        P("fsdp", None),
        P("fsdp", None),
    )
    return jax.shard_map(local, mesh=mesh, in_specs=in_specs, out_specs=out_specs, check_vma=False)
```

profile of v0, /device:TPU:8, one launch (start us, length us, event | category | flops | bytes accessed | tf_op | source)
XLA Modules:
  0.0 420.8 jit_solution(14297391877100147623)
XLA Ops:
  8.0 0.0 all-reduce.4.cloned.1.call-start
  8.7 1.8 convert_subtract_fusion
  10.5 0.0 all-reduce.4.cloned.1.call-update
  10.5 0.0 all-gather.4.cloned.1.call-start
  10.5 0.5 all-gather.4.cloned.1.call-update
  11.1 0.0 reduce-scatter.2.cloned.1.call-start
  11.1 0.7 reduce
  11.9 1.3 fusion.50
  13.9 0.3 dynamic-update-slice
  14.1 80.6 %all-reduce = bf16[5120]{0:T(1024)(128)(2,1)S(1)} all-reduce(bf16[5120]{0:T(1024)(128)(2,1)S(1)} %dynamic-update-slice), channel_id=2, replica_groups=mesh['group'=16,'fsdp'=16] {'fsdp'}, use_global_device_ids=true, to_apply=%add | all-reduce | flops 5120 | bytes 20480
  94.8 0.7 reduce.1
  95.5 0.1 convert_reduce_fusion
  95.6 11.2 %psum.14 = s32[16]{0:T(128)S(1)} all-reduce(s32[16]{0:T(128)S(1)} %convert_reduce_fusion), channel_id=1, replica_groups=mesh['group'=16,'fsdp'=16] {'fsdp'}, use_global_device_ids=true, to_apply=%region_2.0 | all-reduce | flops 16 | bytes 128 | tf_op jit(solution)/shard_map/psum | solution.py:39
  106.7 0.7 bitcast_divide_fusion
  107.4 0.1 select_reduce_fusion
  107.5 2.7 fusion.16
  110.2 10.9 %multiply_convert_fusion = bf16[5120,1024]{1,0:T(8,128)(2,1)} fusion(bf16[1,320,5120]{2,1,0:T(8,128)(2,1)} %param.9, f32[5120]{0:T(1024)S(1)} %convert_element_type.89, f32[320]{0:T(512)S(1)} %add_rsqrt_fusion, bf16[1,320,1024]{2,1,0:T(8,128)(2,1)} %param.10, f32[320]{0:T(512)S(1)} %select_reduce_fusion), kind=kOutput, calls=%fused_computation | convolution fusion | flops 3373465600 | bytes 14440960 | tf_op jit(solution)/shard_map/dot_general | solution.py:63
  121.0 0.0 copy-start
  121.0 0.0 reduce-scatter.2.cloned.1.call-update
  121.8 74.4 %all-reduce.4.cloned.1.call-done = f32[320,256]{1,0:T(8,128)} async-done(((f32[320,256]{1,0:T(8,128)}), f32[320,256]{1,0:T(8,128)}) %all-reduce.4.cloned.1.call-update) | async-done | bytes 327696 | tf_op jit(solution)/shard_map/psum | solution.py:86
  196.2 2.1 multiply_subtract_fusion
  198.3 0.0 all-gather.4.cloned.1.call-done
  198.3 0.0 copy-done
  198.3 11.8 %fusion.15 = (bf16[5120]{0:T(1024)(128)(2,1)S(1)}, f32[320]{0:T(512)S(1)}, f32[320,5120]{1,0:T(8,128)}) fusion(bf16[1,320,5120]{2,1,0:T(8,128)(2,1)S(1)} %copy-done, f32[320]{0:T(512)S(1)} %add_rsqrt_fusion, f32[5120]{0:T(1024)S(1)} %broadcast_multiply_fusion, bf16[1,5120,1024]{2,1,0:T(8,128)(2,1)} %all-gather.4.cloned.1.call-done, ...), kind=kOutput, calls=%fused_computation.18 | convolution fusion | flops 3369528064 | bytes 21006080 | tf_op jit(solution)/shard_map/dot_general | solution.py:50
  210.1 77.6 %all-reduce.1 = bf16[5120]{0:T(1024)(128)(2,1)S(1)} all-reduce(bf16[5120]{0:T(1024)(128)(2,1)S(1)} %get-tuple-element.6), channel_id=5, replica_groups=mesh['group'=16,'fsdp'=16] {'fsdp'}, use_global_device_ids=true, to_apply=%region_7.8.clone | all-reduce | flops 5120 | bytes 20480
  287.8 0.1 dynamic-slice_convert_fusion
  287.8 0.6 reshape.59
  288.4 0.0 copy-start.1
  288.4 7.5 %fusion.40 = bf16[1,320,1024]{2,1,0:T(8,128)(2,1)} fusion(bf16[1,5120,1024]{2,1,0:T(8,128)(2,1)} %all-gather.4.cloned.1.call-done, bf16[1,320,5120]{2,1,0:T(8,128)(2,1)S(1)} %copy-done, f32[5120]{0:T(1024)S(1)} %convert_element_type.89, f32[320]{0:T(512)S(1)} %add_rsqrt_fusion), kind=kOutput, calls=%fused_computation.35 | convolution fusion | flops 3362652160 | bytes 14439680 | tf_op jit(solution)/shard_map/dot_general | solution.py:34
  295.9 0.0 copy-done.1
  295.9 3.8 fusion.21
  299.7 113.7 %reduce-scatter.2.cloned.1.call-done = bf16[320,1024]{1,0:T(8,128)(2,1)} async-done(((bf16[5120,1024]{1,0:T(8,128)(2,1)}), bf16[320,1024]{1,0:T(8,128)(2,1)}) %reduce-scatter.2.cloned.1.call-update) | async-done | bytes 655376 | tf_op jit(solution)/shard_map/reduce_scatter | solution.py:70
  (5 shorter events, 0.0 us)
Async XLA Ops:
  8.0 188.2 %all-reduce.4.cloned.1.call-start = ((), (), s32[]{:S(2)}) async-start(), calls=%async_computation.2 | async-start | bytes 655360 | tf_op jit(solution)/shard_map/psum | solution.py:86
  10.5 187.8 %all-gather.4.cloned.1.call-start = ((), (), s32[]{:S(2)}) async-start(), calls=%async_computation.3 | async-start | bytes 11141120 | tf_op jit(solution)/shard_map/all_gather | solution.py:30
  11.1 402.3 %reduce-scatter.2.cloned.1.call-start = ((), (), s32[]{:S(2)}) async-start(), calls=%async_computation.1 | async-start | bytes 11141120 | tf_op jit(solution)/shard_map/reduce_scatter | solution.py:70
  121.0 77.3 %copy-start = (bf16[1,320,5120]{2,1,0:T(8,128)(2,1)S(1)}, bf16[1,320,5120]{2,1,0:T(8,128)(2,1)}, u32[]{:S(2)}) copy-start(bf16[1,320,5120]{2,1,0:T(8,128)(2,1)} %param.9) | copy-start | bytes 9830404
  288.4 7.5 %copy-start.1 = (f32[320,5120]{1,0:T(8,128)S(1)}, f32[320,5120]{1,0:T(8,128)}, u32[]{:S(2)}) copy-start(f32[320,5120]{1,0:T(8,128)} %get-tuple-element.12) | copy-start | bytes 19660804
Sparse Core Ops, SparseCore 0:
  12.2 183.9 all-reduce.3
Sparse Core Ops, SparseCore 1:
  13.6 160.1 all-gather.3
  178.3 235.1 reduce-scatter.1
where the time goes:
time: 421 us
  waiting for transfers between devices  189 us (45%)
  blocking collectives  169 us (40%)
  matrix products  30.1 us (7%)
  between operations  17.6 us (4%)
  other arithmetic  12.7 us (3%)
    unnamed x2, blocking collectives  158 us
    reduce_scatter x1, waiting for transfers between devices, local(): lax.psum_scatter(weight_term.astype(jnp.bfloat16), 'fsdp', scatter_dimens...  114 us
    psum x1, waiting for transfers between devices, local(): summed = lax.psum(pseudo_term, 'group')  74.4 us
    dot_general x1, matrix products, local(): lax.dot_general(cotangent, lax.all_gather(local_weights[0], 'fsdp', axis=...  11.8 us
    psum x1, blocking collectives, local(): lengths = lax.psum(jnp.sum(onehot.astype(jnp.int32), 0), 'fsdp')  11.2 us
    dot_general x1, matrix products, local(): lax.dot_general(normed, cotangent, (((0,), (0,)), ((), ())), preferred_el...  10.9 us
  transfers between devices with their start and end apart: 3, of which 2 were waited for; matrix products, arithmetic and copies ran while one was open for 10% of the time, Pallas kernels for 0%

commit v1 on v0

v1 whole, which is shorter than its diff:
```python
import functools

import jax
import jax.numpy as jnp
from jax import lax
from jax.experimental import pallas as pl
from jax.experimental.pallas import tpu as pltpu
from jax.sharding import PartitionSpec as P

MESH = pl.DeviceIdType.MESH
F32 = jnp.float32
BF16 = jnp.bfloat16
EPSILON = 1e-06
OUTER_MU = 0.9
OUTER_LR = 0.7
NFRAG = 4
RING = 8
PAIRS = 4
STEPS = 7

GATHER = (
    ((0, 0), (0, 1), (1, 0), (1, 1), (2, 0), (2, 1), (3, 0)),
    ((0, 1), (0, 0), (1, 1), (1, 0), (2, 1), (2, 0), (3, 1)),
)
SCATTER = (
    ((4, 0), (3, 1), (3, 0), (2, 1), (2, 0), (1, 1), (1, 0)),
    ((4, 1), (3, 0), (3, 1), (2, 0), (2, 1), (1, 0), (1, 1)),
)


def to_column(row, n):
    here = lax.broadcasted_iota(jnp.int32, (n, n), 0) == lax.broadcasted_iota(jnp.int32, (n, n), 1)
    return jnp.sum(jnp.where(here, jnp.broadcast_to(row, (n, n)), 0.0), axis=1, keepdims=True)


def to_row(column, n):
    here = lax.broadcasted_iota(jnp.int32, (n, n), 0) == lax.broadcasted_iota(jnp.int32, (n, n), 1)
    return jnp.sum(jnp.where(here, jnp.broadcast_to(column, (n, n)), 0.0), axis=0, keepdims=True)


def kernel(
    inputs, key_grad, seg, adv, gains, weights, outer, moment, frag,
    keys_out, ig_out, wg_out, gg_out, no_out, nm_out,
    x_mine, x_other, w_all, cots, kg, lw, ow, mom, inv, gain_col, weighted,
    u_all, rs_send, rs_recv, sg_mine, sg_send, sg_recv, k_mine, k_send, k_recv,
    ig_buf, k_buf, wg_buf, cnt_own, cnt_recv,
    pg_own, pg_a, pg_s1, pg_b, pg_s2, pg_c, pg_full, pg_e,
    load_sem, store_sem, ag_ss, ag_rs, rs_ss, rs_rs, x_ss, x_rs, cnt_ss, cnt_rs, pg_ss, pg_rs,
):
    tok, width = inputs.shape
    kv = key_grad.shape[1]
    rows = weights.shape[0]
    half = rows // 2
    pair = 2 * rows
    mid = width // 2
    cols = kv // NFRAG
    seqs = adv.shape[1]

    g, f = lax.axis_index("group"), lax.axis_index("fsdp")
    xhi, z = f // RING, lax.rem(f, RING)
    core, y = lax.rem(g, 2), g // 4
    par = lax.rem(z, 2)
    up = xhi * RING + lax.rem(z + 1, RING)
    down = xhi * RING + lax.rem(z + RING - 1, RING)
    across = (1 - xhi) * RING + z
    other_core = g + 1 - 2 * core
    xlo = lax.rem(g // 2, 2)
    side = g + 2 - 4 * xlo
    j = z // 2
    place = (j, lax.rem(j + 3 + 2 * par, 4), lax.rem(j + 1 + 2 * par, 4), lax.rem(j + 2, 4))

    barrier = pltpu.get_barrier_semaphore()
    for i in range(1, 2 * RING):
        pl.semaphore_signal(
            barrier, inc=1, device_id={"fsdp": lax.rem(f + i, 2 * RING)}, device_id_type=MESH
        )
    group_peers = [other_core, side] + [lax.rem(g + 4 * i, 16) for i in (1, 2, 3)]
    for p in group_peers:
        pl.semaphore_signal(barrier, inc=1, device_id={"group": p}, device_id_type=MESH)

    def load(src, dst, i):
        c = pltpu.make_async_copy(src, dst, load_sem.at[i])
        c.start()
        return c

    def col(start):
        return pl.ds(pl.multiple_of(start, 128), pair)

    lw_load = load(weights, lw, 0)
    x_loads = []
    for p in range(PAIRS):
        x_loads.append(load(inputs.at[:, col(xhi * mid + place[p] * pair)], x_mine.at[p, pl.ds(0, tok)], 1 + p))
        x_loads.append(load(inputs.at[:, col((1 - xhi) * mid + place[p] * pair)], x_other.at[p], 5 + p))
    kg_load = load(key_grad, kg, 9)
    ow_load = load(outer, ow, 10)
    mom_load = load(moment, mom, 11)

    seg_col = to_column(seg[...].astype(F32), tok)
    lane = lax.broadcasted_iota(jnp.int32, (tok, 128), 1).astype(F32)
    onehot = jnp.where(jnp.broadcast_to(seg_col, (tok, 128)) == lane, 1.0, 0.0)
    counts = jnp.sum(onehot, axis=0, keepdims=True)
    cnt_own[...] = jnp.broadcast_to(counts, (8, 128))

    gain_col[...] = to_column(gains[...].astype(F32), rows)
    lw_load.wait()
    base = z * rows

    def scale_rows(t, c):
        r = pl.ds(pl.multiple_of(t * 32, 32), 32)
        w_all[pl.ds(pl.multiple_of(base + t * 32, 32), 32)] = (
            lw[r].astype(F32) * gain_col[r]
        ).astype(BF16)
        return c

    lax.fori_loop(0, rows // 32, scale_rows, 0)
    pl.semaphore_wait(barrier, 2 * RING - 1 + len(group_peers))

    def ring_to(way):
        return {"fsdp": up if way == 0 else down}

    def block_rows(way, distance, h, outward):
        sign = 1 if (way == 0) == outward else -1
        b = lax.rem(z + sign * distance + RING, RING)
        return pl.ds(pl.multiple_of(b * rows + h * half, 16), half)

    def gather(way, k):
        distance, h = GATHER[way][k]
        r = block_rows(way, distance, h, False)
        return pltpu.make_async_remote_copy(
            src_ref=w_all.at[r], dst_ref=w_all.at[r], send_sem=ag_ss.at[way, k],
            recv_sem=ag_rs.at[way, k], device_id=ring_to(way), device_id_type=MESH,
        )

    ag = [[gather(way, k) for k in range(STEPS)] for way in (0, 1)]

    def gather_start(k):
        for way in (0, 1):
            ag[way][k].start()

    def gather_step(k):
        for way in (0, 1):
            ag[way][k].wait_recv()
            if k + 2 < STEPS:
                ag[way][k + 2].start()

    gather_start(0)

    cnt = []
    for i in range(1, 2 * RING):
        cnt.append(pltpu.make_async_remote_copy(
            src_ref=cnt_own, dst_ref=cnt_recv.at[i], send_sem=cnt_ss.at[i], recv_sem=cnt_rs.at[i],
            device_id={"fsdp": lax.rem(f + i, 2 * RING)}, device_id_type=MESH,
        ))
        cnt[-1].start()

    def cross(src, dst, i):
        return pltpu.make_async_remote_copy(
            src_ref=src, dst_ref=dst, send_sem=x_ss.at[i], recv_sem=x_rs.at[i],
            device_id={"fsdp": across}, device_id_type=MESH,
        )

    x_cross = [
        cross(inputs.at[:, col((1 - xhi) * mid + place[p] * pair)], x_mine.at[p, pl.ds(tok, tok)], p)
        for p in range(PAIRS)
    ]
    cots_cross = cross(cots.at[pl.ds(0, tok)], cots.at[pl.ds(tok, tok)], 4)
    sg_cross = [cross(sg_send.at[p], sg_recv.at[p], 5 + p) for p in range(PAIRS)]
    k_cross = cross(k_send, k_recv, 9)

    x_cross[3].start()
    gather_start(1)

    chosen = frag[0]

    def pick(ref, r):
        out = ref[r, pl.ds(0, cols)].astype(F32)
        for i in range(1, NFRAG):
            out = jnp.where(chosen == i, ref[r, pl.ds(i * cols, cols)].astype(F32), out)
        return out

    def pick_local(t, c):
        r = pl.ds(pl.multiple_of(t * 32, 32), 32)
        pg_own[r] = pick(lw, r).astype(BF16)
        return c

    lax.fori_loop(0, rows // 32, pick_local, 0)

    def to_group(src, dst, i, peer):
        return pltpu.make_async_remote_copy(
            src_ref=src, dst_ref=dst, send_sem=pg_ss.at[i], recv_sem=pg_rs.at[i],
            device_id={"group": peer}, device_id_type=MESH,
        )

    mine_r = pl.ds(pl.multiple_of(core * half, 16), half)
    theirs_r = pl.ds(pl.multiple_of((1 - core) * half, 16), half)
    quarter = half // 4
    pg_first = to_group(pg_own.at[theirs_r], pg_a, 0, other_core)
    pg_first.start()

    for c in x_loads:
        c.wait()

    def mean_square(t, c):
        r = pl.ds(pl.multiple_of(t * 16, 16), 16)
        total = jnp.zeros((16, pair), F32)
        for p in range(PAIRS):
            a, b = x_mine[p, r].astype(F32), x_other[p, r].astype(F32)
            total = total + a * a + b * b
        inv[r] = lax.rsqrt(jnp.sum(total, axis=1, keepdims=True) * (1.0 / width) + EPSILON)
        return c

    lax.fori_loop(0, tok // 16, mean_square, 0)

    lengths = counts
    for i, c in enumerate(cnt):
        c.wait_recv()
        lengths = lengths + cnt_recv[i + 1, pl.ds(0, 1), :]
    group_tokens = tok * 2 * RING
    per_seq = (
        adv[...] * (group_tokens / seqs)
        / jnp.maximum(lengths[:, :seqs], group_tokens / (2 * seqs))
    )
    token_weight = jnp.sum(onehot[:, :seqs] * per_seq, axis=1, keepdims=True)
    weighted[...] = token_weight * inv[...] * (width ** -0.5)
    kg_load.wait()

    def scale_tokens(t, c):
        r = pl.ds(pl.multiple_of(t * 32, 32), 32)
        cots[r] = (kg[r].astype(F32) * weighted[r]).astype(BF16)
        return c

    lax.fori_loop(0, tok // 32, scale_tokens, 0)
    cots_cross.start()
    x_cross[2].start()

    n_tile = 256

    def u_pair(p):
        across_t = x_mine[p].T

        def body(n, c):
            at = pl.ds(pl.multiple_of(n * n_tile, n_tile), n_tile)
            u_all[pl.ds(pl.multiple_of(place[p] * pair, 16), pair), at] = jnp.dot(
                across_t, cots[:, at], preferred_element_type=F32
            )
            return c

        lax.fori_loop(0, kv // n_tile, body, 0)

    def sg_part(p, r):
        w = w_all[pl.ds(pl.multiple_of(place[p] * pair, 16), pair)]
        return lax.dot_general(
            cots[r], w, (((1,), (1,)), ((), ())), preferred_element_type=F32
        )

    def sg_theirs(p):
        sg_send[p] = sg_part(p, pl.ds(tok, tok)).astype(BF16)
        sg_cross[p].start()

    def sg_ours(p):
        sg_mine[p] = sg_part(p, pl.ds(0, tok))

    def keys_half(first, out, kind):
        def body(n, c):
            at = pl.ds(pl.multiple_of(n * n_tile, n_tile), n_tile)
            total = jnp.zeros((tok, n_tile), F32)
            for p in range(PAIRS):
                total = total + jnp.dot(
                    x_mine[p, pl.ds(first, tok)],
                    w_all[pl.ds(pl.multiple_of(place[p] * pair, 16), pair), at],
                    preferred_element_type=F32,
                )
            out[:, at] = total.astype(kind)
            return c

        lax.fori_loop(0, kv // n_tile, body, 0)

    def scatter(way, k):
        return pltpu.make_async_remote_copy(
            src_ref=rs_send.at[way, k], dst_ref=rs_recv.at[way, k], send_sem=rs_ss.at[way, k],
            recv_sem=rs_rs.at[way, k], device_id=ring_to(way), device_id_type=MESH,
        )

    rs = [[scatter(way, k) for k in range(STEPS)] for way in (0, 1)]

    def scatter_send(k):
        for way in (0, 1):
            distance, h = SCATTER[way][k]
            b = block_rows(way, distance, h, True)
            if k >= 2:
                rs[way][k - 2].wait_recv()

            def body(t, c, way=way, b=b, k=k):
                r = pl.ds(pl.multiple_of(t * 32, 32), 32)
                term = u_all[pl.ds(pl.multiple_of(b.start + t * 32, 32), 32)]
                if k >= 2:
                    term = term + rs_recv[way, k - 2, r].astype(F32)
                rs_send[way, k, r] = term.astype(BF16)
                return c

            lax.fori_loop(0, half // 32, body, 0)
            rs[way][k].start()

    gather_step(0)
    pg_first.wait_recv()
    pg_s1[...] = pg_own[mine_r].astype(F32) + pg_a[...].astype(F32)
    pg_second = []
    for i in (1, 2, 3):
        yy = lax.rem(y + i, 4)
        pg_second.append(to_group(
            pg_s1.at[pl.ds(pl.multiple_of(yy * quarter, 8), quarter)], pg_b.at[i], i, lax.rem(g + 4 * i, 16)
        ))
        pg_second[-1].start()
    gather_step(1)
    x_cross[1].start()
    for c in pg_second:
        c.wait_recv()
    own_q = pl.ds(pl.multiple_of(y * quarter, 8), quarter)
    pg_s2[...] = pg_s1[own_q] + pg_b[1] + pg_b[2] + pg_b[3]
    pg_third = to_group(pg_s2, pg_c, 4, side)
    pg_third.start()
    gather_step(2)
    x_cross[0].start()
    pg_third.wait_recv()
    pg_full[own_q] = pg_s2[...] + pg_c[...]
    pg_fourth = []
    for i in (1, 2, 3):
        pg_fourth.append(to_group(pg_full.at[own_q], pg_full.at[own_q], 4 + i, lax.rem(g + 4 * i, 16)))
        pg_fourth[-1].start()
    cots_cross.wait_recv()
    x_cross[3].wait_recv()
    u_pair(3)
    gather_step(3)
    sg_theirs(0)
    for c in pg_fourth:
        c.wait_recv()
    pg_fifth = to_group(pg_full, pg_e, 8, other_core)
    pg_fifth.start()
    x_cross[2].wait_recv()
    u_pair(2)
    gather_step(4)
    scatter_send(0)
    scatter_send(1)
    sg_theirs(1)
    x_cross[1].wait_recv()
    u_pair(1)
    gather_step(5)
    sg_theirs(2)
    gather_step(6)
    sg_theirs(3)
    scatter_send(2)
    x_cross[0].wait_recv()
    u_pair(0)
    scatter_send(3)
    keys_half(tok, k_send, BF16)
    k_cross.start()
    sg_ours(0)
    scatter_send(4)
    sg_ours(1)
    sg_ours(2)
    scatter_send(5)
    sg_ours(3)

    pg_fifth.wait_recv()
    ow_load.wait()
    mom_load.wait()

    def outer_half(r, total_ref):
        def body(t, c):
            rr = pl.ds(pl.multiple_of(r.start + t * 32, 32), 32)
            o, m = pick(ow, rr), pick(mom, rr)
            pseudo = o - total_ref[pl.ds(pl.multiple_of(t * 32, 32), 32)] * (1.0 / 16)
            new_m = OUTER_MU * m + pseudo
            nm_out[rr] = new_m
            no_out[rr] = o - OUTER_LR * (pseudo + OUTER_MU * new_m)
            return c

        lax.fori_loop(0, half // 32, body, 0)

    outer_half(mine_r, pg_full)
    outer_half(theirs_r, pg_e)
    scatter_send(6)
    keys_half(0, k_mine, F32)

    for p in (0, 1, 2, 3):
        sg_cross[p].wait_recv()

    def finish_rows(t, c):
        r = pl.ds(pl.multiple_of(t * 16, 16), 16)
        total = jnp.zeros((16, pair), F32)
        for p in range(PAIRS):
            total = total + sg_mine[p, r] * x_mine[p, r].astype(F32)
            total = total + sg_recv[p, r].astype(F32) * x_other[p, r].astype(F32)
        i = inv[r]
        m = jnp.sum(total, axis=1, keepdims=True) * (1.0 / width) * i * i
        for p in range(PAIRS):
            ig_buf[p, r] = (sg_mine[p, r] - m * x_mine[p, r].astype(F32)).astype(BF16)
            ig_buf[PAIRS + p, r] = (
                sg_recv[p, r].astype(F32) - m * x_other[p, r].astype(F32)
            ).astype(BF16)
        return c

    lax.fori_loop(0, tok // 16, finish_rows, 0)
    stores = []

    def store(src, dst, i):
        c = pltpu.make_async_copy(src, dst, store_sem.at[i])
        c.start()
        stores.append(c)

    for p in range(PAIRS):
        store(ig_buf.at[p], ig_out.at[:, col(xhi * mid + place[p] * pair)], p)
        store(ig_buf.at[PAIRS + p], ig_out.at[:, col((1 - xhi) * mid + place[p] * pair)], PAIRS + p)

    k_cross.wait_recv()

    def finish_keys(t, c):
        r = pl.ds(pl.multiple_of(t * 32, 32), 32)
        k_buf[r] = ((k_mine[r] + k_recv[r].astype(F32)) * (inv[r] * (width ** -0.5))).astype(BF16)
        return c

    lax.fori_loop(0, tok // 32, finish_keys, 0)
    store(k_buf, keys_out, 8)

    for k in (5, 6):
        for way in (0, 1):
            rs[way][k].wait_recv()
    gain_sum = []
    for h in (0, 1):
        k_up, k_down = (6, 5) if h == 0 else (5, 6)

        def body(t, c, h=h, k_up=k_up, k_down=k_down):
            r = pl.ds(pl.multiple_of(t * 32, 32), 32)
            rr = pl.ds(pl.multiple_of(h * half + t * 32, 32), 32)
            total = u_all[pl.ds(pl.multiple_of(base + h * half + t * 32, 32), 32)]
            total = total + rs_recv[0, k_up, r].astype(F32) + rs_recv[1, k_down, r].astype(F32)
            wg_buf[rr] = (total * gain_col[rr]).astype(BF16)
            weighted[rr] = jnp.sum(total * lw[rr].astype(F32), axis=1, keepdims=True)
            return c

        lax.fori_loop(0, half // 32, body, 0)
    store(wg_buf, wg_out, 9)
    gg_out[...] = to_row(weighted[...], rows)

    for c in stores:
        c.wait()
    for way in (0, 1):
        for k in range(STEPS):
            ag[way][k].wait_send()
            rs[way][k].wait_send()
    for c in cnt + x_cross + sg_cross + [cots_cross, k_cross, pg_first, pg_third, pg_fifth]:
        c.wait_send()
    for c in pg_second + pg_fourth:
        c.wait_send()


def local(
    inputs, key_grad, seg_ids, advantages, gains, local_weights, outer_weights, momentum, frag_index
):
    tok, width = inputs.shape[1:]
    kv, rows = key_grad.shape[2], local_weights.shape[1]
    half, pair, cols = rows // 2, 2 * rows, kv // NFRAG
    hbm, vmem = pl.BlockSpec(memory_space=pl.ANY), pl.BlockSpec(memory_space=pltpu.VMEM)
    dma = pltpu.SemaphoreType.DMA
    scratch = [
        pltpu.VMEM((PAIRS, 2 * tok, pair), BF16),
        pltpu.VMEM((PAIRS, tok, pair), BF16),
        pltpu.VMEM((RING * rows, kv), BF16),
        pltpu.VMEM((2 * tok, kv), BF16),
        pltpu.VMEM((tok, kv), BF16),
        pltpu.VMEM((rows, kv), BF16),
        pltpu.VMEM((rows, kv), F32),
        pltpu.VMEM((rows, kv), F32),
        pltpu.VMEM((tok, 1), F32),
        pltpu.VMEM((rows, 1), F32),
        pltpu.VMEM((tok, 1), F32),
        pltpu.VMEM((RING * rows, kv), F32),
        pltpu.VMEM((2, STEPS, half, kv), BF16),
        pltpu.VMEM((2, STEPS, half, kv), BF16),
        pltpu.VMEM((PAIRS, tok, pair), F32),
        pltpu.VMEM((PAIRS, tok, pair), BF16),
        pltpu.VMEM((PAIRS, tok, pair), BF16),
        pltpu.VMEM((tok, kv), F32),
        pltpu.VMEM((tok, kv), BF16),
        pltpu.VMEM((tok, kv), BF16),
        pltpu.VMEM((2 * PAIRS, tok, pair), BF16),
        pltpu.VMEM((tok, kv), BF16),
        pltpu.VMEM((rows, kv), BF16),
        pltpu.VMEM((8, 128), F32),
        pltpu.VMEM((2 * RING, 8, 128), F32),
        pltpu.VMEM((rows, cols), BF16),
        pltpu.VMEM((half, cols), BF16),
        pltpu.VMEM((half, cols), F32),
        pltpu.VMEM((4, half // 4, cols), F32),
        pltpu.VMEM((half // 4, cols), F32),
        pltpu.VMEM((half // 4, cols), F32),
        pltpu.VMEM((half, cols), F32),
        pltpu.VMEM((half, cols), F32),
        dma((12,)), dma((10,)),
        dma((2, STEPS)), dma((2, STEPS)), dma((2, STEPS)), dma((2, STEPS)),
        dma((10,)), dma((10,)), dma((2 * RING,)), dma((2 * RING,)), dma((9,)), dma((9,)),
    ]
    flops = 6 * 2 * tok * (width // 2) * kv
    out = pl.pallas_call(
        kernel,
        out_shape=[
            jax.ShapeDtypeStruct((tok, kv), BF16),
            jax.ShapeDtypeStruct((tok, width), BF16),
            jax.ShapeDtypeStruct((rows, kv), BF16),
            jax.ShapeDtypeStruct((1, rows), F32),
            jax.ShapeDtypeStruct((rows, cols), F32),
            jax.ShapeDtypeStruct((rows, cols), F32),
        ],
        in_specs=[
            hbm, hbm, vmem, vmem, vmem, hbm, hbm, hbm, pl.BlockSpec(memory_space=pltpu.SMEM),
        ],
        out_specs=[hbm, hbm, hbm, vmem, vmem, vmem],
        scratch_shapes=scratch,
        compiler_params=pltpu.CompilerParams(
            collective_id=0, has_side_effects=True, vmem_limit_bytes=62 * 2**20
        ),
        cost_estimate=pl.CostEstimate(flops=flops, bytes_accessed=20 * 2**20, transcendentals=0),
        name="key_projection",
    )(
        inputs[0], key_grad[0], seg_ids, advantages, gains, local_weights[0],
        outer_weights, momentum, frag_index,
    )
    keys, input_grad, weight_grad, gain_grad, new_outer, new_momentum = out
    return keys[None], input_grad[None], weight_grad[None], gain_grad, new_outer, new_momentum


def solution(mesh):
    in_specs = (
        P("group", "fsdp", None),
        P("group", "fsdp", None),
        P("group", "fsdp"),
        P("group", None),
        P("group", "fsdp"),
        P("group", "fsdp", None),
        P("fsdp", None),
        P("fsdp", None),
        P(),
    )
    out_specs = (
        P("group", "fsdp", None),
        P("group", "fsdp", None),
        P("group", "fsdp", None),
        P("group", "fsdp"),
        P("fsdp", None),
        P("fsdp", None),
    )
    return jax.shard_map(local, mesh=mesh, in_specs=in_specs, out_specs=out_specs, check_vma=False)
```

time: 421 us -> 136 us (0.32)
  waiting for transfers between devices: 189 us -> 0 us
  blocking collectives: 169 us -> 0 us
  Pallas kernels: 0 us -> 126 us
  matrix products: 30.1 us -> 0 us
  between operations: 17.6 us -> 1.3 us
  other arithmetic: 12.7 us -> 0 us
  local copies, waits for them, and re-layouts: 2.18 us -> 8.77 us
    unnamed x2 -> x0, blocking collectives: 158 us -> none
    pallas_call x0 -> x1, Pallas kernels: none -> 126 us  [local(): pl.pallas_call(kernel, out_shape=[jax.ShapeDtypeStruct((tok, kv), BF16),...]
    reduce_scatter x1 -> x0, waiting for transfers between devices: 114 us -> none  [local(): lax.psum_scatter(weight_term.astype(jnp.bfloat16), 'fsdp', scatter_dimens...]
    psum x1 -> x0, waiting for transfers between devices: 74.4 us -> none  [local(): summed = lax.psum(pseudo_term, 'group')]
    dot_general x3 -> x0, matrix products: 30.1 us -> none  [the longest x1 11.8 us: local(): lax.dot_general(cotangent, lax.all_gather(local_weights[0], 'fsdp', axis=...]
    psum x1 -> x0, blocking collectives: 11.2 us -> none  [local(): lengths = lax.psum(jnp.sum(onehot.astype(jnp.int32), 0), 'fsdp')]
    unnamed x7 -> x14, local copies, waits for them, and re-layouts: 1.61 us -> 8.77 us
  transfers between devices with their start and end apart: 3 -> 0, of which waited for: 2 -> 0; matrix products, arithmetic and copies ran while one was open for 10% -> 0% of each run, Pallas kernels for 0% -> 0%
where the time goes in v1:
time: 136 us
  Pallas kernels  126 us (93%)
  local copies, waits for them, and re-layouts  8.77 us (6%)
    pallas_call x1, Pallas kernels, local(): pl.pallas_call(kernel, out_shape=[jax.ShapeDtypeStruct((tok, kv), BF16),...  126 us
    unnamed x14, local copies, waits for them, and re-layouts  8.77 us

profile of v1, /device:TPU:8, one launch (start us, length us, event | category | flops | bytes accessed | tf_op | source)
XLA Modules:
  0.0 135.9 jit_solution(6723373591542310911)
XLA Ops:
  1.3 125.8 %key_projection.1 = (bf16[320,1024]{1,0:T(8,128)(2,1)}, bf16[320,5120]{1,0:T(8,128)(2,1)}, bf16[320,1024]{1,0:T(8,128)(2,1)}, f32[1,320]{1,0:T(1,128)}, f32[320,256]{1,0:T(8,128)}, /*index=5*/f32[320,256]{1,0:T(8,128)}) custom-call(bf16[320,5120]{1,0:T(8,128)(2,1)} %bitcast.9, bf16[320,1024]{1,0:T(8,128)(2,1)} %bitcast.10, s32[1,320]{1,0:T(1,128)} %seg.1, ...), custom_call_target="tpu_custom_call" | custom-call | flops 10066329600 | bytes 20971520 | tf_op jit(solution)/shard_map/key_projection/pallas_call | solution.py:504
  127.1 2.0 %copy.22 = bf16[1,320,1024]{2,1,0:T(8,128)(2,1)} copy(bf16[1,320,1024]{2,1,0:T(8,128)(2,1)} %bitcast.8) | data formatting | bytes 1310720
  129.1 0.0 copy-start
  129.1 0.0 copy-start.3
  129.1 0.0 copy-start.2
  129.1 0.0 copy-start.1
  129.1 3.9 %copy.23 = bf16[1,320,5120]{2,1,0:T(8,128)(2,1)} copy(bf16[1,320,5120]{2,1,0:T(8,128)(2,1)} %bitcast.6) | data formatting | bytes 6553600
  133.0 0.0 copy-done
  133.0 0.8 copy.24
  133.9 0.0 copy-done.3
  133.9 0.6 copy.25
  134.4 0.0 copy-done.2
  134.5 0.7 copy.26
  135.2 0.0 copy-done.1
  135.2 0.7 copy.27
Async XLA Ops:
  129.1 4.0 %copy-start = (bf16[320,1024]{1,0:T(8,128)(2,1)S(1)}, bf16[320,1024]{1,0:T(8,128)(2,1)}, u32[]{:S(2)}) copy-start(bf16[320,1024]{1,0:T(8,128)(2,1)} %get-tuple-element.14) | copy-start | bytes 1966084
  129.1 4.8 %copy-start.3 = (f32[1,320]{1,0:T(1,128)S(1)}, f32[1,320]{1,0:T(1,128)}, u32[]{:S(2)}) copy-start(f32[1,320]{1,0:T(1,128)} %get-tuple-element.27) | copy-start | bytes 3844
  129.1 5.4 %copy-start.2 = (f32[320,256]{1,0:T(8,128)S(1)}, f32[320,256]{1,0:T(8,128)}, u32[]{:S(2)}) copy-start(f32[320,256]{1,0:T(8,128)} %get-tuple-element.28) | copy-start | bytes 983044
  129.1 6.1 %copy-start.1 = (f32[320,256]{1,0:T(8,128)S(1)}, f32[320,256]{1,0:T(8,128)}, u32[]{:S(2)}) copy-start(f32[320,256]{1,0:T(8,128)} %get-tuple-element.29) | copy-start | bytes 983044

commit v2 on v1

--- a/solution.py
+++ b/solution.py
@@ -39,13 +39,12 @@
 
 
 def kernel(
-    inputs, key_grad, seg, adv, gains, weights, outer, moment, frag,
-    keys_out, ig_out, wg_out, gg_out, no_out, nm_out,
-    x_mine, x_other, w_all, cots, kg, lw, ow, mom, inv, gain_col, weighted,
+    inputs, key_grad, seg, adv, gains, weights, frag,
+    k_buf, ig_buf, wg_buf, gg_out, pg_total,
+    x_mine, x_other, w_all, cots, kg, lw, inv, gain_col, weighted,
     u_all, rs_send, rs_recv, sg_mine, sg_send, sg_recv, k_mine, k_send, k_recv,
-    ig_buf, k_buf, wg_buf, cnt_own, cnt_recv,
-    pg_own, pg_a, pg_s1, pg_b, pg_s2, pg_c, pg_full, pg_e,
-    load_sem, store_sem, ag_ss, ag_rs, rs_ss, rs_rs, x_ss, x_rs, cnt_ss, cnt_rs, pg_ss, pg_rs,
+    cnt_own, cnt_recv, pg_own, pg_a, pg_s1, pg_b, pg_s2, pg_c,
+    load_sem, ag_ss, ag_rs, rs_ss, rs_rs, x_ss, x_rs, cnt_ss, cnt_rs, pg_ss, pg_rs,
 ):
     tok, width = inputs.shape
     kv = key_grad.shape[1]
@@ -54,29 +53,32 @@
     pair = 2 * rows
     mid = width // 2
     cols = kv // NFRAG
+    quarter = rows // 4
     seqs = adv.shape[1]
 
     g, f = lax.axis_index("group"), lax.axis_index("fsdp")
     xhi, z = f // RING, lax.rem(f, RING)
-    core, y = lax.rem(g, 2), g // 4
     par = lax.rem(z, 2)
     up = xhi * RING + lax.rem(z + 1, RING)
     down = xhi * RING + lax.rem(z + RING - 1, RING)
     across = (1 - xhi) * RING + z
+    core, y = lax.rem(g, 2), g // 4
+    side = g + 2 - 4 * lax.rem(g // 2, 2)
     other_core = g + 1 - 2 * core
-    xlo = lax.rem(g // 2, 2)
-    side = g + 2 - 4 * xlo
+    over_y = [lax.rem(g + 4 * i, 16) for i in (1, 2, 3)]
     j = z // 2
     place = (j, lax.rem(j + 3 + 2 * par, 4), lax.rem(j + 1 + 2 * par, 4), lax.rem(j + 2, 4))
 
     barrier = pltpu.get_barrier_semaphore()
-    for i in range(1, 2 * RING):
-        pl.semaphore_signal(
-            barrier, inc=1, device_id={"fsdp": lax.rem(f + i, 2 * RING)}, device_id_type=MESH
-        )
-    group_peers = [other_core, side] + [lax.rem(g + 4 * i, 16) for i in (1, 2, 3)]
-    for p in group_peers:
-        pl.semaphore_signal(barrier, inc=1, device_id={"group": p}, device_id_type=MESH)
+    ring = [xhi * RING + lax.rem(z + i, RING) for i in range(1, RING)]
+    for peer in ring + [across]:
+        pl.semaphore_signal(barrier, inc=1, device_id={"fsdp": peer}, device_id_type=MESH)
+    for peer in over_y + [side]:
+        pl.semaphore_signal(barrier, inc=1, device_id={"group": peer}, device_id_type=MESH)
+
+    @pl.when(core == 0)
+    def _():
+        pl.semaphore_signal(barrier, inc=1, device_id={"group": other_core}, device_id_type=MESH)
 
     def load(src, dst, i):
         c = pltpu.make_async_copy(src, dst, load_sem.at[i])
@@ -92,14 +94,6 @@
         x_loads.append(load(inputs.at[:, col(xhi * mid + place[p] * pair)], x_mine.at[p, pl.ds(0, tok)], 1 + p))
         x_loads.append(load(inputs.at[:, col((1 - xhi) * mid + place[p] * pair)], x_other.at[p], 5 + p))
     kg_load = load(key_grad, kg, 9)
-    ow_load = load(outer, ow, 10)
-    mom_load = load(moment, mom, 11)
-
-    seg_col = to_column(seg[...].astype(F32), tok)
-    lane = lax.broadcasted_iota(jnp.int32, (tok, 128), 1).astype(F32)
-    onehot = jnp.where(jnp.broadcast_to(seg_col, (tok, 128)) == lane, 1.0, 0.0)
-    counts = jnp.sum(onehot, axis=0, keepdims=True)
-    cnt_own[...] = jnp.broadcast_to(counts, (8, 128))
 
     gain_col[...] = to_column(gains[...].astype(F32), rows)
     lw_load.wait()
@@ -113,7 +107,7 @@
         return c
 
     lax.fori_loop(0, rows // 32, scale_rows, 0)
-    pl.semaphore_wait(barrier, 2 * RING - 1 + len(group_peers))
+    pl.semaphore_wait(barrier, RING + 4 + core)
 
     def ring_to(way):
         return {"fsdp": up if way == 0 else down}
@@ -143,16 +137,6 @@
             if k + 2 < STEPS:
                 ag[way][k + 2].start()
 
-    gather_start(0)
-
-    cnt = []
-    for i in range(1, 2 * RING):
-        cnt.append(pltpu.make_async_remote_copy(
-            src_ref=cnt_own, dst_ref=cnt_recv.at[i], send_sem=cnt_ss.at[i], recv_sem=cnt_rs.at[i],
-            device_id={"fsdp": lax.rem(f + i, 2 * RING)}, device_id_type=MESH,
-        ))
-        cnt[-1].start()
-
     def cross(src, dst, i):
         return pltpu.make_async_remote_copy(
             src_ref=src, dst_ref=dst, send_sem=x_ss.at[i], recv_sem=x_rs.at[i],
@@ -167,23 +151,36 @@
     sg_cross = [cross(sg_send.at[p], sg_recv.at[p], 5 + p) for p in range(PAIRS)]
     k_cross = cross(k_send, k_recv, 9)
 
+    gather_start(0)
     x_cross[3].start()
     gather_start(1)
 
+    seg_col = to_column(seg[...].astype(F32), tok)
+    lane = lax.broadcasted_iota(jnp.int32, (tok, 128), 1).astype(F32)
+    onehot = jnp.where(jnp.broadcast_to(seg_col, (tok, 128)) == lane, 1.0, 0.0)
+    counts = jnp.sum(onehot, axis=0, keepdims=True)
+    cnt_own[0] = jnp.broadcast_to(counts, (8, 128))
+
+    def count_copy(src, dst, i, peer):
+        c = pltpu.make_async_remote_copy(
+            src_ref=src, dst_ref=dst, send_sem=cnt_ss.at[i], recv_sem=cnt_rs.at[i],
+            device_id={"fsdp": peer}, device_id_type=MESH,
+        )
+        c.start()
+        return c
+
+    cnt = [count_copy(cnt_own.at[0], cnt_recv.at[0], 0, across)]
+    x_cross[2].start()
+
     chosen = frag[0]
 
-    def pick(ref, r):
-        out = ref[r, pl.ds(0, cols)].astype(F32)
+    def pick_rows(t, c):
+        r = pl.ds(pl.multiple_of(t * 32, 32), 32)
+        out = lw[r, pl.ds(0, cols)].astype(F32)
         for i in range(1, NFRAG):
-            out = jnp.where(chosen == i, ref[r, pl.ds(i * cols, cols)].astype(F32), out)
-        return out
-
-    def pick_local(t, c):
-        r = pl.ds(pl.multiple_of(t * 32, 32), 32)
-        pg_own[r] = pick(lw, r).astype(BF16)
-        return c
-
-    lax.fori_loop(0, rows // 32, pick_local, 0)
+            out = jnp.where(chosen == i, lw[r, pl.ds(i * cols, cols)].astype(F32), out)
+        pg_own[r] = out.astype(BF16)
+        return c
 
     def to_group(src, dst, i, peer):
         return pltpu.make_async_remote_copy(
@@ -191,11 +188,18 @@
             device_id={"group": peer}, device_id_type=MESH,
         )
 
-    mine_r = pl.ds(pl.multiple_of(core * half, 16), half)
-    theirs_r = pl.ds(pl.multiple_of((1 - core) * half, 16), half)
-    quarter = half // 4
-    pg_first = to_group(pg_own.at[theirs_r], pg_a, 0, other_core)
-    pg_first.start()
+    def rows_of(yy):
+        return pl.ds(pl.multiple_of(yy * quarter, 16), quarter)
+
+    pg_first = [
+        to_group(pg_own.at[rows_of(lax.rem(y + i, 4))], pg_a.at[i], i, over_y[i - 1]) for i in (1, 2, 3)
+    ]
+    pg_second = to_group(pg_s1, pg_b, 4, side)
+    pg_third = to_group(pg_s2, pg_c, 5, other_core)
+    pg_last = [
+        to_group(pg_total.at[rows_of(y)], pg_total.at[rows_of(y)], 5 + i, over_y[i - 1])
+        for i in (1, 2, 3)
+    ]
 
     for c in x_loads:
         c.wait()
@@ -210,11 +214,28 @@
         return c
 
     lax.fori_loop(0, tok // 16, mean_square, 0)
-
-    lengths = counts
-    for i, c in enumerate(cnt):
+    lax.fori_loop(0, rows // 32, pick_rows, 0)
+    for c in pg_first:
+        c.start()
+
+    gather_step(0)
+    cnt[0].wait_recv()
+    cnt_own[1] = cnt_own[0] + cnt_recv[0]
+    for i in range(1, RING):
+        cnt.append(count_copy(cnt_own.at[1], cnt_recv.at[i], i, ring[i - 1]))
+    for c in pg_first:
         c.wait_recv()
-        lengths = lengths + cnt_recv[i + 1, pl.ds(0, 1), :]
+    pg_s1[...] = (
+        pg_own[rows_of(y)].astype(F32) + pg_a[1].astype(F32) + pg_a[2].astype(F32)
+        + pg_a[3].astype(F32)
+    )
+    pg_second.start()
+    gather_step(1)
+    lengths = cnt_own[1, pl.ds(0, 1), :]
+    for i in range(1, RING):
+        cnt[i].wait_recv()
+        lengths = lengths + cnt_recv[i, pl.ds(0, 1), :]
+
     group_tokens = tok * 2 * RING
     per_seq = (
         adv[...] * (group_tokens / seqs)
@@ -231,7 +252,6 @@
 
     lax.fori_loop(0, tok // 32, scale_tokens, 0)
     cots_cross.start()
-    x_cross[2].start()
 
     n_tile = 256
 
@@ -301,57 +321,51 @@
             lax.fori_loop(0, half // 32, body, 0)
             rs[way][k].start()
 
-    gather_step(0)
-    pg_first.wait_recv()
-    pg_s1[...] = pg_own[mine_r].astype(F32) + pg_a[...].astype(F32)
-    pg_second = []
-    for i in (1, 2, 3):
-        yy = lax.rem(y + i, 4)
-        pg_second.append(to_group(
-            pg_s1.at[pl.ds(pl.multiple_of(yy * quarter, 8), quarter)], pg_b.at[i], i, lax.rem(g + 4 * i, 16)
-        ))
-        pg_second[-1].start()
-    gather_step(1)
+    gather_step(2)
     x_cross[1].start()
-    for c in pg_second:
-        c.wait_recv()
-    own_q = pl.ds(pl.multiple_of(y * quarter, 8), quarter)
-    pg_s2[...] = pg_s1[own_q] + pg_b[1] + pg_b[2] + pg_b[3]
-    pg_third = to_group(pg_s2, pg_c, 4, side)
-    pg_third.start()
-    gather_step(2)
+    pg_second.wait_recv()
+    pg_s2[...] = pg_s1[...] + pg_b[...]
+
+    @pl.when(core == 1)
+    def _():
+        pg_third.start()
+
+    gather_step(3)
     x_cross[0].start()
-    pg_third.wait_recv()
-    pg_full[own_q] = pg_s2[...] + pg_c[...]
-    pg_fourth = []
-    for i in (1, 2, 3):
-        pg_fourth.append(to_group(pg_full.at[own_q], pg_full.at[own_q], 4 + i, lax.rem(g + 4 * i, 16)))
-        pg_fourth[-1].start()
+    gather_step(4)
+    x_cross[3].wait_recv()
     cots_cross.wait_recv()
-    x_cross[3].wait_recv()
     u_pair(3)
-    gather_step(3)
-    sg_theirs(0)
-    for c in pg_fourth:
-        c.wait_recv()
-    pg_fifth = to_group(pg_full, pg_e, 8, other_core)
-    pg_fifth.start()
+    scatter_send(0)
     x_cross[2].wait_recv()
     u_pair(2)
-    gather_step(4)
-    scatter_send(0)
     scatter_send(1)
+    sg_theirs(0)
+    gather_step(5)
     sg_theirs(1)
+
+    @pl.when(core == 0)
+    def _():
+        pg_third.wait_recv()
+        pg_third.start()
+
     x_cross[1].wait_recv()
     u_pair(1)
-    gather_step(5)
+    gather_step(6)
     sg_theirs(2)
-    gather_step(6)
+    scatter_send(2)
     sg_theirs(3)
-    scatter_send(2)
     x_cross[0].wait_recv()
     u_pair(0)
     scatter_send(3)
+
+    @pl.when(core == 1)
+    def _():
+        pg_third.wait_recv()
+
+    pg_total[rows_of(y)] = pg_s2[...] + pg_c[...]
+    for c in pg_last:
+        c.start()
     keys_half(tok, k_send, BF16)
     k_cross.start()
     sg_ours(0)
@@ -360,27 +374,10 @@
     sg_ours(2)
     scatter_send(5)
     sg_ours(3)
-
-    pg_fifth.wait_recv()
-    ow_load.wait()
-    mom_load.wait()
-
-    def outer_half(r, total_ref):
-        def body(t, c):
-            rr = pl.ds(pl.multiple_of(r.start + t * 32, 32), 32)
-            o, m = pick(ow, rr), pick(mom, rr)
-            pseudo = o - total_ref[pl.ds(pl.multiple_of(t * 32, 32), 32)] * (1.0 / 16)
-            new_m = OUTER_MU * m + pseudo
-            nm_out[rr] = new_m
-            no_out[rr] = o - OUTER_LR * (pseudo + OUTER_MU * new_m)
-            return c
-
-        lax.fori_loop(0, half // 32, body, 0)
-
-    outer_half(mine_r, pg_full)
-    outer_half(theirs_r, pg_e)
     scatter_send(6)
     keys_half(0, k_mine, F32)
+    for c in pg_last:
+        c.wait_recv()
 
     for p in (0, 1, 2, 3):
         sg_cross[p].wait_recv()
@@ -394,23 +391,13 @@
         i = inv[r]
         m = jnp.sum(total, axis=1, keepdims=True) * (1.0 / width) * i * i
         for p in range(PAIRS):
-            ig_buf[p, r] = (sg_mine[p, r] - m * x_mine[p, r].astype(F32)).astype(BF16)
-            ig_buf[PAIRS + p, r] = (
+            ig_buf[r, col(xhi * mid + place[p] * pair)] = (sg_mine[p, r] - m * x_mine[p, r].astype(F32)).astype(BF16)
+            ig_buf[r, col((1 - xhi) * mid + place[p] * pair)] = (
                 sg_recv[p, r].astype(F32) - m * x_other[p, r].astype(F32)
             ).astype(BF16)
         return c
 
     lax.fori_loop(0, tok // 16, finish_rows, 0)
-    stores = []
-
-    def store(src, dst, i):
-        c = pltpu.make_async_copy(src, dst, store_sem.at[i])
-        c.start()
-        stores.append(c)
-
-    for p in range(PAIRS):
-        store(ig_buf.at[p], ig_out.at[:, col(xhi * mid + place[p] * pair)], p)
-        store(ig_buf.at[PAIRS + p], ig_out.at[:, col((1 - xhi) * mid + place[p] * pair)], PAIRS + p)
 
     k_cross.wait_recv()
 
@@ -420,7 +407,6 @@
         return c
 
     lax.fori_loop(0, tok // 32, finish_keys, 0)
-    store(k_buf, keys_out, 8)
 
     for k in (5, 6):
         for way in (0, 1):
@@ -439,19 +425,46 @@
             return c
 
         lax.fori_loop(0, half // 32, body, 0)
-    store(wg_buf, wg_out, 9)
     gg_out[...] = to_row(weighted[...], rows)
 
-    for c in stores:
-        c.wait()
     for way in (0, 1):
         for k in range(STEPS):
             ag[way][k].wait_send()
             rs[way][k].wait_send()
-    for c in cnt + x_cross + sg_cross + [cots_cross, k_cross, pg_first, pg_third, pg_fifth]:
+    for c in cnt + x_cross + sg_cross + pg_first + pg_last + [cots_cross, k_cross, pg_second, pg_third]:
         c.wait_send()
-    for c in pg_second + pg_fourth:
-        c.wait_send()
+
+
+def finish(
+    keys, ig, wg, gg, total, outer, moment, frag,
+    keys_out, ig_out, wg_out, gg_out, no_out, nm_out,
+    o, m, new_o, new_m, sem,
+):
+    rows, cols = o.shape
+    at = pl.ds(pl.multiple_of(frag[0] * cols, cols), cols)
+    copies = [
+        pltpu.make_async_copy(outer.at[:, at], o, sem.at[0]),
+        pltpu.make_async_copy(moment.at[:, at], m, sem.at[1]),
+        pltpu.make_async_copy(ig, ig_out, sem.at[2]),
+        pltpu.make_async_copy(keys, keys_out, sem.at[3]),
+        pltpu.make_async_copy(wg, wg_out, sem.at[4]),
+        pltpu.make_async_copy(gg, gg_out, sem.at[5]),
+    ]
+    for c in copies:
+        c.start()
+    copies[0].wait()
+    copies[1].wait()
+    pseudo = o[...] - total[...] * (1.0 / 16)
+    new_m[...] = OUTER_MU * m[...] + pseudo
+    new_o[...] = o[...] - OUTER_LR * (pseudo + OUTER_MU * new_m[...])
+    last = [
+        pltpu.make_async_copy(new_o, no_out, sem.at[6]),
+        pltpu.make_async_copy(new_m, nm_out, sem.at[7]),
+    ]
+    for c in last:
+        c.start()
+    for c in copies[2:] + last:
+        c.wait()
 
 
 def local(
@@ -460,7 +473,8 @@
     tok, width = inputs.shape[1:]
     kv, rows = key_grad.shape[2], local_weights.shape[1]
     half, pair, cols = rows // 2, 2 * rows, kv // NFRAG
-    hbm, vmem = pl.BlockSpec(memory_space=pl.ANY), pl.BlockSpec(memory_space=pltpu.VMEM)
+    hbm, vmem = pl.BlockSpec(memory_space=pltpu.HBM), pl.BlockSpec(memory_space=pltpu.VMEM)
+    smem = pl.BlockSpec(memory_space=pltpu.SMEM)
     dma = pltpu.SemaphoreType.DMA
     scratch = [
         pltpu.VMEM((PAIRS, 2 * tok, pair), BF16),
@@ -469,8 +483,6 @@
         pltpu.VMEM((2 * tok, kv), BF16),
         pltpu.VMEM((tok, kv), BF16),
         pltpu.VMEM((rows, kv), BF16),
-        pltpu.VMEM((rows, kv), F32),
-        pltpu.VMEM((rows, kv), F32),
         pltpu.VMEM((tok, 1), F32),
         pltpu.VMEM((rows, 1), F32),
         pltpu.VMEM((tok, 1), F32),
@@ -483,26 +495,40 @@
         pltpu.VMEM((tok, kv), F32),
         pltpu.VMEM((tok, kv), BF16),
         pltpu.VMEM((tok, kv), BF16),
-        pltpu.VMEM((2 * PAIRS, tok, pair), BF16),
-        pltpu.VMEM((tok, kv), BF16),
-        pltpu.VMEM((rows, kv), BF16),
-        pltpu.VMEM((8, 128), F32),
-        pltpu.VMEM((2 * RING, 8, 128), F32),
+        pltpu.VMEM((2, 8, 128), F32),
+        pltpu.VMEM((RING, 8, 128), F32),
         pltpu.VMEM((rows, cols), BF16),
-        pltpu.VMEM((half, cols), BF16),
-        pltpu.VMEM((half, cols), F32),
-        pltpu.VMEM((4, half // 4, cols), F32),
-        pltpu.VMEM((half // 4, cols), F32),
-        pltpu.VMEM((half // 4, cols), F32),
-        pltpu.VMEM((half, cols), F32),
-        pltpu.VMEM((half, cols), F32),
-        dma((12,)), dma((10,)),
-        dma((2, STEPS)), dma((2, STEPS)), dma((2, STEPS)), dma((2, STEPS)),
-        dma((10,)), dma((10,)), dma((2 * RING,)), dma((2 * RING,)), dma((9,)), dma((9,)),
+        pltpu.VMEM((4, rows // 4, cols), BF16),
+        pltpu.VMEM((rows // 4, cols), F32),
+        pltpu.VMEM((rows // 4, cols), F32),
+        pltpu.VMEM((rows // 4, cols), F32),
+        pltpu.VMEM((rows // 4, cols), F32),
+        dma((10,)), dma((2, STEPS)), dma((2, STEPS)), dma((2, STEPS)), dma((2, STEPS)),
+        dma((10,)), dma((10,)), dma((RING,)), dma((RING,)), dma((9,)), dma((9,)),
     ]
     flops = 6 * 2 * tok * (width // 2) * kv
-    out = pl.pallas_call(
+    keys, input_grad, weight_grad, gain_grad, total = pl.pallas_call(
         kernel,
+        out_shape=[
+            pltpu.VMEM((tok, kv), BF16),
+            pltpu.VMEM((tok, width), BF16),
+            pltpu.VMEM((rows, kv), BF16),
+            pltpu.VMEM((1, rows), F32),
+            pltpu.VMEM((rows, cols), F32),
+        ],
+        in_specs=[hbm, hbm, vmem, vmem, vmem, hbm, smem],
+        out_specs=[vmem] * 5,
+        scratch_shapes=scratch,
+        compiler_params=pltpu.CompilerParams(
+            collective_id=0, has_side_effects=True, vmem_limit_bytes=52 * 2**20
+        ),
+        cost_estimate=pl.CostEstimate(
+            flops=10 * flops, bytes_accessed=200 * 2**20, transcendentals=0
+        ),
+        name="key_projection",
+    )(inputs[0], key_grad[0], seg_ids, advantages, gains, local_weights[0], frag_index)
+    keys, input_grad, weight_grad, gain_grad, new_outer, new_momentum = pl.pallas_call(
+        finish,
         out_shape=[
             jax.ShapeDtypeStruct((tok, kv), BF16),
             jax.ShapeDtypeStruct((tok, width), BF16),
@@ -511,21 +537,12 @@
             jax.ShapeDtypeStruct((rows, cols), F32),
             jax.ShapeDtypeStruct((rows, cols), F32),
         ],
-        in_specs=[
-            hbm, hbm, vmem, vmem, vmem, hbm, hbm, hbm, pl.BlockSpec(memory_space=pltpu.SMEM),
-        ],
-        out_specs=[hbm, hbm, hbm, vmem, vmem, vmem],
-        scratch_shapes=scratch,
-        compiler_params=pltpu.CompilerParams(
-            collective_id=0, has_side_effects=True, vmem_limit_bytes=62 * 2**20
-        ),
-        cost_estimate=pl.CostEstimate(flops=flops, bytes_accessed=20 * 2**20, transcendentals=0),
-        name="key_projection",
-    )(
-        inputs[0], key_grad[0], seg_ids, advantages, gains, local_weights[0],
-        outer_weights, momentum, frag_index,
-    )
-    keys, input_grad, weight_grad, gain_grad, new_outer, new_momentum = out
+        in_specs=[vmem] * 5 + [hbm, hbm, smem],
+        out_specs=[hbm] * 6,
+        scratch_shapes=[pltpu.VMEM((rows, cols), F32)] * 4 + [dma((8,))],
+        compiler_params=pltpu.CompilerParams(vmem_limit_bytes=16 * 2**20),
+        name="finish",
+    )(keys, input_grad, weight_grad, gain_grad, total, outer_weights, momentum, frag_index)
     return keys[None], input_grad[None], weight_grad[None], gain_grad, new_outer, new_momentum
 
 

time: 136 us -> 124 us (0.912)
  local copies, waits for them, and re-layouts: 8.77 us -> 0.01 us
  Pallas kernels: 126 us -> 122 us
    unnamed x14 -> x4, local copies, waits for them, and re-layouts: 8.77 us -> 0.01 us
    pallas_call x1 -> x2, Pallas kernels: 126 us -> 122 us  [the longest x1 120 us: local(): pl.pallas_call(kernel, out_shape=[pltpu.VMEM((tok, kv), BF16), pltpu.VMEM...]
where the time goes in v2:
time: 124 us
  Pallas kernels  122 us (98%)
  between operations  1.32 us (1%)
    pallas_call x1, Pallas kernels, local(): pl.pallas_call(kernel, out_shape=[pltpu.VMEM((tok, kv), BF16), pltpu.VMEM...  120 us

profile of v2, /device:TPU:8, one launch (start us, length us, event | category | flops | bytes accessed | tf_op | source)
XLA Modules:
  0.0 123.6 jit_solution(15529967792496127330)
XLA Ops:
  1.3 0.0 copy-start
  1.3 0.0 copy-start.1
  1.3 119.8 %key_projection.1 = (bf16[320,1024]{1,0:T(8,128)(2,1)S(1)}, bf16[320,5120]{1,0:T(8,128)(2,1)S(1)}, bf16[320,1024]{1,0:T(8,128)(2,1)S(1)}, f32[1,320]{1,0:T(1,128)S(1)}, f32[320,256]{1,0:T(8,128)S(1)}) custom-call(bf16[320,5120]{1,0:T(8,128)(2,1)} %bitcast.6, bf16[320,1024]{1,0:T(8,128)(2,1)} %bitcast.8, s32[1,320]{1,0:T(1,128)} %seg.1, f32[1,16]{1,0:T(1,128)} %adv.1, ...), custom_call_target="tpu_custom_call" | custom-call | flops 100663296000 | bytes 209715200 | tf_op jit(solution)/shard_map/key_projection/pallas_call | solution.py:510
  121.1 0.0 copy-done
  121.1 0.0 copy-done.1
  121.1 2.5 %finish.1 = (bf16[320,1024]{1,0:T(8,128)(2,1)}, bf16[320,5120]{1,0:T(8,128)(2,1)}, bf16[320,1024]{1,0:T(8,128)(2,1)}, f32[1,320]{1,0:T(1,128)}, f32[320,256]{1,0:T(8,128)}, /*index=5*/f32[320,256]{1,0:T(8,128)}) custom-call(bf16[320,1024]{1,0:T(8,128)(2,1)S(1)} %get-tuple-element.17.keys, bf16[320,5120]{1,0:T(8,128)(2,1)S(1)} %get-tuple-element.18.ig, ...), custom_call_target="tpu_custom_call" | custom-call | tf_op jit(solution)/shard_map/finish/pallas_call | solution.py:530
Async XLA Ops:
  1.3 119.8 %copy-start = (f32[320,1024]{1,0:T(8,128)S(1)}, f32[320,1024]{1,0:T(8,128)}, u32[]{:S(2)}) copy-start(f32[320,1024]{1,0:T(8,128)} %outer.1) | copy-start | bytes 3932164
  1.3 119.8 %copy-start.1 = (f32[320,1024]{1,0:T(8,128)S(1)}, f32[320,1024]{1,0:T(8,128)}, u32[]{:S(2)}) copy-start(f32[320,1024]{1,0:T(8,128)} %moment.1) | copy-start | bytes 3932164

commit v3 on v2

--- a/solution.py
+++ b/solution.py
@@ -69,6 +69,16 @@
     j = z // 2
     place = (j, lax.rem(j + 3 + 2 * par, 4), lax.rem(j + 1 + 2 * par, 4), lax.rem(j + 2, 4))
 
+    def load(src, dst, i):
+        c = pltpu.make_async_copy(src, dst, load_sem.at[i])
+        c.start()
+        return c
+
+    def col(start):
+        return pl.ds(pl.multiple_of(start, 128), pair)
+
+    lw_load = load(weights, lw, 0)
+
     barrier = pltpu.get_barrier_semaphore()
     ring = [xhi * RING + lax.rem(z + i, RING) for i in range(1, RING)]
     for peer in ring + [across]:
@@ -79,21 +89,6 @@
     @pl.when(core == 0)
     def _():
         pl.semaphore_signal(barrier, inc=1, device_id={"group": other_core}, device_id_type=MESH)
-
-    def load(src, dst, i):
-        c = pltpu.make_async_copy(src, dst, load_sem.at[i])
-        c.start()
-        return c
-
-    def col(start):
-        return pl.ds(pl.multiple_of(start, 128), pair)
-
-    lw_load = load(weights, lw, 0)
-    x_loads = []
-    for p in range(PAIRS):
-        x_loads.append(load(inputs.at[:, col(xhi * mid + place[p] * pair)], x_mine.at[p, pl.ds(0, tok)], 1 + p))
-        x_loads.append(load(inputs.at[:, col((1 - xhi) * mid + place[p] * pair)], x_other.at[p], 5 + p))
-    kg_load = load(key_grad, kg, 9)
 
     gain_col[...] = to_column(gains[...].astype(F32), rows)
     lw_load.wait()
@@ -149,11 +144,18 @@
     ]
     cots_cross = cross(cots.at[pl.ds(0, tok)], cots.at[pl.ds(tok, tok)], 4)
     sg_cross = [cross(sg_send.at[p], sg_recv.at[p], 5 + p) for p in range(PAIRS)]
-    k_cross = cross(k_send, k_recv, 9)
+    k_cross = [
+        cross(k_send.at[pl.ds(h * half, half)], k_recv.at[pl.ds(h * half, half)], 9 + h) for h in (0, 1)
+    ]
 
     gather_start(0)
     x_cross[3].start()
     gather_start(1)
+    x_loads = []
+    for p in range(PAIRS):
+        x_loads.append(load(inputs.at[:, col(xhi * mid + place[p] * pair)], x_mine.at[p, pl.ds(0, tok)], 1 + p))
+        x_loads.append(load(inputs.at[:, col((1 - xhi) * mid + place[p] * pair)], x_other.at[p], 5 + p))
+    kg_load = load(key_grad, kg, 9)
 
     seg_col = to_column(seg[...].astype(F32), tok)
     lane = lax.broadcasted_iota(jnp.int32, (tok, 128), 1).astype(F32)
@@ -201,8 +203,6 @@
         for i in (1, 2, 3)
     ]
 
-    for c in x_loads:
-        c.wait()
 
     def mean_square(t, c):
         r = pl.ds(pl.multiple_of(t * 16, 16), 16)
@@ -213,24 +213,18 @@
         inv[r] = lax.rsqrt(jnp.sum(total, axis=1, keepdims=True) * (1.0 / width) + EPSILON)
         return c
 
-    lax.fori_loop(0, tok // 16, mean_square, 0)
-    lax.fori_loop(0, rows // 32, pick_rows, 0)
-    for c in pg_first:
-        c.start()
-
-    gather_step(0)
+
     cnt[0].wait_recv()
     cnt_own[1] = cnt_own[0] + cnt_recv[0]
     for i in range(1, RING):
         cnt.append(count_copy(cnt_own.at[1], cnt_recv.at[i], i, ring[i - 1]))
+    for c in x_loads:
+        c.wait()
+    lax.fori_loop(0, tok // 16, mean_square, 0)
+    gather_step(0)
+    lax.fori_loop(0, rows // 32, pick_rows, 0)
     for c in pg_first:
-        c.wait_recv()
-    pg_s1[...] = (
-        pg_own[rows_of(y)].astype(F32) + pg_a[1].astype(F32) + pg_a[2].astype(F32)
-        + pg_a[3].astype(F32)
-    )
-    pg_second.start()
-    gather_step(1)
+        c.start()
     lengths = cnt_own[1, pl.ds(0, 1), :]
     for i in range(1, RING):
         cnt[i].wait_recv()
@@ -252,6 +246,7 @@
 
     lax.fori_loop(0, tok // 32, scale_tokens, 0)
     cots_cross.start()
+    gather_step(1)
 
     n_tile = 256
 
@@ -321,6 +316,13 @@
             lax.fori_loop(0, half // 32, body, 0)
             rs[way][k].start()
 
+    for c in pg_first:
+        c.wait_recv()
+    pg_s1[...] = (
+        pg_own[rows_of(y)].astype(F32) + pg_a[1].astype(F32) + pg_a[2].astype(F32)
+        + pg_a[3].astype(F32)
+    )
+    pg_second.start()
     gather_step(2)
     x_cross[1].start()
     pg_second.wait_recv()
@@ -367,7 +369,8 @@
     for c in pg_last:
         c.start()
     keys_half(tok, k_send, BF16)
-    k_cross.start()
+    for c in k_cross:
+        c.start()
     sg_ours(0)
     scatter_send(4)
     sg_ours(1)
@@ -378,6 +381,12 @@
     keys_half(0, k_mine, F32)
     for c in pg_last:
         c.wait_recv()
+
+    for way in (0, 1):
+        for k in range(STEPS):
+            ag[way][k].wait_send()
+    for c in cnt + x_cross + pg_first + pg_last + [cots_cross, pg_second, pg_third]:
+        c.wait_send()
 
     for p in (0, 1, 2, 3):
         sg_cross[p].wait_recv()
@@ -399,39 +408,54 @@
 
     lax.fori_loop(0, tok // 16, finish_rows, 0)
 
-    k_cross.wait_recv()
-
-    def finish_keys(t, c):
-        r = pl.ds(pl.multiple_of(t * 32, 32), 32)
-        k_buf[r] = ((k_mine[r] + k_recv[r].astype(F32)) * (inv[r] * (width ** -0.5))).astype(BF16)
-        return c
-
-    lax.fori_loop(0, tok // 32, finish_keys, 0)
-
-    for k in (5, 6):
-        for way in (0, 1):
-            rs[way][k].wait_recv()
-    gain_sum = []
-    for h in (0, 1):
-        k_up, k_down = (6, 5) if h == 0 else (5, 6)
-
-        def body(t, c, h=h, k_up=k_up, k_down=k_down):
+    def add_own(h, way, k):
+        rs[way][k].wait_recv()
+
+        def body(t, c):
             r = pl.ds(pl.multiple_of(t * 32, 32), 32)
-            rr = pl.ds(pl.multiple_of(h * half + t * 32, 32), 32)
-            total = u_all[pl.ds(pl.multiple_of(base + h * half + t * 32, 32), 32)]
-            total = total + rs_recv[0, k_up, r].astype(F32) + rs_recv[1, k_down, r].astype(F32)
+            rr = pl.ds(pl.multiple_of(base + h * half + t * 32, 32), 32)
+            u_all[rr] = u_all[rr] + rs_recv[way, k, r].astype(F32)
+            return c
+
+        lax.fori_loop(0, half // 32, body, 0)
+
+    add_own(1, 0, 5)
+    add_own(0, 1, 5)
+    for way in (0, 1):
+        for k in range(STEPS - 1):
+            rs[way][k].wait_send()
+    for c in sg_cross:
+        c.wait_send()
+
+    def finish_keys(h):
+        k_cross[h].wait_recv()
+
+        def body(t, c):
+            r = pl.ds(pl.multiple_of(h * half + t * 32, 32), 32)
+            k_buf[r] = ((k_mine[r] + k_recv[r].astype(F32)) * (inv[r] * (width ** -0.5))).astype(BF16)
+            return c
+
+        lax.fori_loop(0, half // 32, body, 0)
+
+    finish_keys(0)
+
+    for way in (0, 1):
+        rs[way][6].wait_recv()
+
+        def body(t, c, way=way):
+            r = pl.ds(pl.multiple_of(t * 32, 32), 32)
+            rr = pl.ds(pl.multiple_of(way * half + t * 32, 32), 32)
+            total = u_all[pl.ds(pl.multiple_of(base + way * half + t * 32, 32), 32)]
+            total = total + rs_recv[way, 6, r].astype(F32)
             wg_buf[rr] = (total * gain_col[rr]).astype(BF16)
             weighted[rr] = jnp.sum(total * lw[rr].astype(F32), axis=1, keepdims=True)
             return c
 
         lax.fori_loop(0, half // 32, body, 0)
     gg_out[...] = to_row(weighted[...], rows)
-
-    for way in (0, 1):
-        for k in range(STEPS):
-            ag[way][k].wait_send()
-            rs[way][k].wait_send()
-    for c in cnt + x_cross + sg_cross + pg_first + pg_last + [cots_cross, k_cross, pg_second, pg_third]:
+    finish_keys(1)
+
+    for c in k_cross + [rs[0][6], rs[1][6]]:
         c.wait_send()
 
 
@@ -504,7 +528,7 @@
         pltpu.VMEM((rows // 4, cols), F32),
         pltpu.VMEM((rows // 4, cols), F32),
         dma((10,)), dma((2, STEPS)), dma((2, STEPS)), dma((2, STEPS)), dma((2, STEPS)),
-        dma((10,)), dma((10,)), dma((RING,)), dma((RING,)), dma((9,)), dma((9,)),
+        dma((11,)), dma((11,)), dma((RING,)), dma((RING,)), dma((9,)), dma((9,)),
     ]
     flops = 6 * 2 * tok * (width // 2) * kv
     keys, input_grad, weight_grad, gain_grad, total = pl.pallas_call(

time: 124 us -> 117 us (0.944)
  Pallas kernels: 122 us -> 116 us
    pallas_call x1, Pallas kernels: 120 us -> 113 us  [local(): pl.pallas_call(kernel, out_shape=[pltpu.VMEM((tok, kv), BF16), pltpu.VMEM...]
where the time goes in v3:
time: 117 us
  Pallas kernels  116 us (99%)
  between operations  1.32 us (1%)
    pallas_call x1, Pallas kernels, local(): pl.pallas_call(kernel, out_shape=[pltpu.VMEM((tok, kv), BF16), pltpu.VMEM...  113 us
    pallas_call x1, Pallas kernels, local(): pl.pallas_call(finish, out_shape=[jax.ShapeDtypeStruct((tok, kv), BF16),...  2.47 us

profile of v3, /device:TPU:8, one launch (start us, length us, event | category | flops | bytes accessed | tf_op | source)
XLA Modules:
  0.0 117.3 jit_solution(5914350194071146439)
XLA Ops:
  1.3 0.0 copy-start
  1.3 0.0 copy-start.1
  1.3 113.5 %key_projection.1 = (bf16[320,1024]{1,0:T(8,128)(2,1)S(1)}, bf16[320,5120]{1,0:T(8,128)(2,1)S(1)}, bf16[320,1024]{1,0:T(8,128)(2,1)S(1)}, f32[1,320]{1,0:T(1,128)S(1)}, f32[320,256]{1,0:T(8,128)S(1)}) custom-call(bf16[320,5120]{1,0:T(8,128)(2,1)} %bitcast.6, bf16[320,1024]{1,0:T(8,128)(2,1)} %bitcast.8, s32[1,320]{1,0:T(1,128)} %seg.1, f32[1,16]{1,0:T(1,128)} %adv.1, ...), custom_call_target="tpu_custom_call" | custom-call | flops 100663296000 | bytes 209715200 | tf_op jit(solution)/shard_map/key_projection/pallas_call | solution.py:534
  114.8 0.0 copy-done
  114.8 0.0 copy-done.1
  114.8 2.5 %finish.1 = (bf16[320,1024]{1,0:T(8,128)(2,1)}, bf16[320,5120]{1,0:T(8,128)(2,1)}, bf16[320,1024]{1,0:T(8,128)(2,1)}, f32[1,320]{1,0:T(1,128)}, f32[320,256]{1,0:T(8,128)}, /*index=5*/f32[320,256]{1,0:T(8,128)}) custom-call(bf16[320,1024]{1,0:T(8,128)(2,1)S(1)} %get-tuple-element.17.keys, bf16[320,5120]{1,0:T(8,128)(2,1)S(1)} %get-tuple-element.18.ig, ...), custom_call_target="tpu_custom_call" | custom-call | tf_op jit(solution)/shard_map/finish/pallas_call | solution.py:554
Async XLA Ops:
  1.3 113.5 %copy-start = (f32[320,1024]{1,0:T(8,128)S(1)}, f32[320,1024]{1,0:T(8,128)}, u32[]{:S(2)}) copy-start(f32[320,1024]{1,0:T(8,128)} %outer.1) | copy-start | bytes 3932164
  1.3 113.5 %copy-start.1 = (f32[320,1024]{1,0:T(8,128)S(1)}, f32[320,1024]{1,0:T(8,128)}, u32[]{:S(2)}) copy-start(f32[320,1024]{1,0:T(8,128)} %moment.1) | copy-start | bytes 3932164

commit v4 on v3

--- a/solution.py
+++ b/solution.py
@@ -39,10 +39,10 @@
 
 
 def kernel(
-    inputs, key_grad, seg, adv, gains, weights, frag,
+    inputs, key_grad, seg_in, adv_in, gains_in, weights, frag,
     k_buf, ig_buf, wg_buf, gg_out, pg_total,
     x_mine, x_other, w_all, cots, kg, lw, inv, gain_col, weighted,
-    u_all, rs_send, rs_recv, sg_mine, sg_send, sg_recv, k_mine, k_send, k_recv,
+    seg, adv, gains, u_all, rs_send, rs_recv, sg_mine, sg_send, sg_recv, k_mine, k_send, k_recv,
     cnt_own, cnt_recv, pg_own, pg_a, pg_s1, pg_b, pg_s2, pg_c,
     load_sem, ag_ss, ag_rs, rs_ss, rs_rs, x_ss, x_rs, cnt_ss, cnt_rs, pg_ss, pg_rs,
 ):
@@ -54,7 +54,7 @@
     mid = width // 2
     cols = kv // NFRAG
     quarter = rows // 4
-    seqs = adv.shape[1]
+    seqs = adv_in.shape[1]
 
     g, f = lax.axis_index("group"), lax.axis_index("fsdp")
     xhi, z = f // RING, lax.rem(f, RING)
@@ -77,7 +77,10 @@
     def col(start):
         return pl.ds(pl.multiple_of(start, 128), pair)
 
+    gain_load = load(gains_in, gains, 10)
     lw_load = load(weights, lw, 0)
+    seg_load = load(seg_in, seg, 11)
+    adv_load = load(adv_in, adv, 12)
 
     barrier = pltpu.get_barrier_semaphore()
     ring = [xhi * RING + lax.rem(z + i, RING) for i in range(1, RING)]
@@ -90,6 +93,7 @@
     def _():
         pl.semaphore_signal(barrier, inc=1, device_id={"group": other_core}, device_id_type=MESH)
 
+    gain_load.wait()
     gain_col[...] = to_column(gains[...].astype(F32), rows)
     lw_load.wait()
     base = z * rows
@@ -157,6 +161,7 @@
         x_loads.append(load(inputs.at[:, col((1 - xhi) * mid + place[p] * pair)], x_other.at[p], 5 + p))
     kg_load = load(key_grad, kg, 9)
 
+    seg_load.wait()
     seg_col = to_column(seg[...].astype(F32), tok)
     lane = lax.broadcasted_iota(jnp.int32, (tok, 128), 1).astype(F32)
     onehot = jnp.where(jnp.broadcast_to(seg_col, (tok, 128)) == lane, 1.0, 0.0)
@@ -230,6 +235,7 @@
         cnt[i].wait_recv()
         lengths = lengths + cnt_recv[i, pl.ds(0, 1), :]
 
+    adv_load.wait()
     group_tokens = tok * 2 * RING
     per_seq = (
         adv[...] * (group_tokens / seqs)
@@ -462,32 +468,35 @@
 def finish(
     keys, ig, wg, gg, total, outer, moment, frag,
     keys_out, ig_out, wg_out, gg_out, no_out, nm_out,
-    o, m, new_o, new_m, sem,
+    new_o, new_m, sem,
 ):
-    rows, cols = o.shape
+    rows, cols = new_o.shape
+    tok = ig.shape[0]
+    part = tok // 4
     at = pl.ds(pl.multiple_of(frag[0] * cols, cols), cols)
     copies = [
-        pltpu.make_async_copy(outer.at[:, at], o, sem.at[0]),
-        pltpu.make_async_copy(moment.at[:, at], m, sem.at[1]),
-        pltpu.make_async_copy(ig, ig_out, sem.at[2]),
-        pltpu.make_async_copy(keys, keys_out, sem.at[3]),
-        pltpu.make_async_copy(wg, wg_out, sem.at[4]),
-        pltpu.make_async_copy(gg, gg_out, sem.at[5]),
+        pltpu.make_async_copy(
+            ig.at[pl.ds(i * part, part)], ig_out.at[pl.ds(i * part, part)], sem.at[i]
+        )
+        for i in range(4)
+    ] + [
+        pltpu.make_async_copy(keys, keys_out, sem.at[4]),
+        pltpu.make_async_copy(wg, wg_out, sem.at[5]),
+        pltpu.make_async_copy(gg, gg_out, sem.at[6]),
     ]
     for c in copies:
         c.start()
-    copies[0].wait()
-    copies[1].wait()
-    pseudo = o[...] - total[...] * (1.0 / 16)
-    new_m[...] = OUTER_MU * m[...] + pseudo
-    new_o[...] = o[...] - OUTER_LR * (pseudo + OUTER_MU * new_m[...])
+    o, m = outer[:, at], moment[:, at]
+    pseudo = o - total[...] * (1.0 / 16)
+    new_m[...] = OUTER_MU * m + pseudo
+    new_o[...] = o - OUTER_LR * (pseudo + OUTER_MU * new_m[...])
     last = [
-        pltpu.make_async_copy(new_o, no_out, sem.at[6]),
-        pltpu.make_async_copy(new_m, nm_out, sem.at[7]),
+        pltpu.make_async_copy(new_o, no_out, sem.at[7]),
+        pltpu.make_async_copy(new_m, nm_out, sem.at[8]),
     ]
     for c in last:
         c.start()
-    for c in copies[2:] + last:
+    for c in copies + last:
         c.wait()
 
 
@@ -510,6 +519,9 @@
         pltpu.VMEM((tok, 1), F32),
         pltpu.VMEM((rows, 1), F32),
         pltpu.VMEM((tok, 1), F32),
+        pltpu.VMEM(seg_ids.shape, seg_ids.dtype),
+        pltpu.VMEM(advantages.shape, F32),
+        pltpu.VMEM(gains.shape, gains.dtype),
         pltpu.VMEM((RING * rows, kv), F32),
         pltpu.VMEM((2, STEPS, half, kv), BF16),
         pltpu.VMEM((2, STEPS, half, kv), BF16),
@@ -527,7 +539,7 @@
         pltpu.VMEM((rows // 4, cols), F32),
         pltpu.VMEM((rows // 4, cols), F32),
         pltpu.VMEM((rows // 4, cols), F32),
-        dma((10,)), dma((2, STEPS)), dma((2, STEPS)), dma((2, STEPS)), dma((2, STEPS)),
+        dma((13,)), dma((2, STEPS)), dma((2, STEPS)), dma((2, STEPS)), dma((2, STEPS)),
         dma((11,)), dma((11,)), dma((RING,)), dma((RING,)), dma((9,)), dma((9,)),
     ]
     flops = 6 * 2 * tok * (width // 2) * kv
@@ -540,7 +552,7 @@
             pltpu.VMEM((1, rows), F32),
             pltpu.VMEM((rows, cols), F32),
         ],
-        in_specs=[hbm, hbm, vmem, vmem, vmem, hbm, smem],
+        in_specs=[hbm] * 6 + [smem],
         out_specs=[vmem] * 5,
         scratch_shapes=scratch,
         compiler_params=pltpu.CompilerParams(
@@ -561,9 +573,9 @@
             jax.ShapeDtypeStruct((rows, cols), F32),
             jax.ShapeDtypeStruct((rows, cols), F32),
         ],
-        in_specs=[vmem] * 5 + [hbm, hbm, smem],
+        in_specs=[vmem] * 7 + [smem],
         out_specs=[hbm] * 6,
-        scratch_shapes=[pltpu.VMEM((rows, cols), F32)] * 4 + [dma((8,))],
+        scratch_shapes=[pltpu.VMEM((rows, cols), F32)] * 2 + [dma((9,))],
         compiler_params=pltpu.CompilerParams(vmem_limit_bytes=16 * 2**20),
         name="finish",
     )(keys, input_grad, weight_grad, gain_grad, total, outer_weights, momentum, frag_index)

time: 117 us -> 117 us (level)
  no operation moved by 1% of the time
where the time goes in v4:
time: 117 us; the launch traced here: 116 us
  Pallas kernels  115 us (98%)
  between operations  1.32 us (1%)
    pallas_call x1, Pallas kernels, local(): pl.pallas_call(kernel, out_shape=[pltpu.VMEM((tok, kv), BF16), pltpu.VMEM...  113 us
    pallas_call x1, Pallas kernels, local(): pl.pallas_call(finish, out_shape=[jax.ShapeDtypeStruct((tok, kv), BF16),...  2.42 us

profile of v4, /device:TPU:8, one launch (start us, length us, event | category | flops | bytes accessed | tf_op | source)
XLA Modules:
  0.0 116.5 jit_solution(17820376161390824774)
XLA Ops:
  1.3 0.0 copy-start
  1.3 0.0 copy-start.1
  1.3 112.7 %key_projection.1 = (bf16[320,1024]{1,0:T(8,128)(2,1)S(1)}, bf16[320,5120]{1,0:T(8,128)(2,1)S(1)}, bf16[320,1024]{1,0:T(8,128)(2,1)S(1)}, f32[1,320]{1,0:T(1,128)S(1)}, f32[320,256]{1,0:T(8,128)S(1)}) custom-call(bf16[320,5120]{1,0:T(8,128)(2,1)} %bitcast.6, bf16[320,1024]{1,0:T(8,128)(2,1)} %bitcast.8, s32[1,320]{1,0:T(1,128)} %seg_in.1, f32[1,16]{1,0:T(1,128)} %adv_in.1, ...), custom_call_target="tpu_custom_call" | custom-call | flops 100663296000 | bytes 209715200 | tf_op jit(solution)/shard_map/key_projection/pallas_call | solution.py:546
  114.0 0.0 copy-done
  114.0 0.0 copy-done.1
  114.1 2.4 %finish.1 = (bf16[320,1024]{1,0:T(8,128)(2,1)}, bf16[320,5120]{1,0:T(8,128)(2,1)}, bf16[320,1024]{1,0:T(8,128)(2,1)}, f32[1,320]{1,0:T(1,128)}, f32[320,256]{1,0:T(8,128)}, /*index=5*/f32[320,256]{1,0:T(8,128)}) custom-call(bf16[320,1024]{1,0:T(8,128)(2,1)S(1)} %get-tuple-element.17.keys, bf16[320,5120]{1,0:T(8,128)(2,1)S(1)} %get-tuple-element.18.ig, ...), custom_call_target="tpu_custom_call" | custom-call | tf_op jit(solution)/shard_map/finish/pallas_call | solution.py:566
Async XLA Ops:
  1.3 112.8 %copy-start = (f32[320,1024]{1,0:T(8,128)S(1)}, f32[320,1024]{1,0:T(8,128)}, u32[]{:S(2)}) copy-start(f32[320,1024]{1,0:T(8,128)} %outer.1) | copy-start | bytes 3932164
  1.3 112.8 %copy-start.1 = (f32[320,1024]{1,0:T(8,128)S(1)}, f32[320,1024]{1,0:T(8,128)}, u32[]{:S(2)}) copy-start(f32[320,1024]{1,0:T(8,128)} %moment.1) | copy-start | bytes 3932164

commit v5 on v4

--- a/solution.py
+++ b/solution.py
@@ -95,6 +95,12 @@
 
     gain_load.wait()
     gain_col[...] = to_column(gains[...].astype(F32), rows)
+    seg_load.wait()
+    seg_col = to_column(seg[...].astype(F32), tok)
+    lane = lax.broadcasted_iota(jnp.int32, (tok, 128), 1).astype(F32)
+    onehot = jnp.where(jnp.broadcast_to(seg_col, (tok, 128)) == lane, 1.0, 0.0)
+    counts = jnp.sum(onehot, axis=0, keepdims=True)
+    cnt_own[0] = jnp.broadcast_to(counts, (8, 128))
     lw_load.wait()
     base = z * rows
 
@@ -107,6 +113,16 @@
 
     lax.fori_loop(0, rows // 32, scale_rows, 0)
     pl.semaphore_wait(barrier, RING + 4 + core)
+
+    def count_copy(src, dst, i, peer):
+        c = pltpu.make_async_remote_copy(
+            src_ref=src, dst_ref=dst, send_sem=cnt_ss.at[i], recv_sem=cnt_rs.at[i],
+            device_id={"fsdp": peer}, device_id_type=MESH,
+        )
+        c.start()
+        return c
+
+    cnt = [count_copy(cnt_own.at[0], cnt_recv.at[0], 0, across)]
 
     def ring_to(way):
         return {"fsdp": up if way == 0 else down}
@@ -154,30 +170,12 @@
 
     gather_start(0)
     x_cross[3].start()
-    gather_start(1)
     x_loads = []
     for p in range(PAIRS):
         x_loads.append(load(inputs.at[:, col(xhi * mid + place[p] * pair)], x_mine.at[p, pl.ds(0, tok)], 1 + p))
         x_loads.append(load(inputs.at[:, col((1 - xhi) * mid + place[p] * pair)], x_other.at[p], 5 + p))
     kg_load = load(key_grad, kg, 9)
 
-    seg_load.wait()
-    seg_col = to_column(seg[...].astype(F32), tok)
-    lane = lax.broadcasted_iota(jnp.int32, (tok, 128), 1).astype(F32)
-    onehot = jnp.where(jnp.broadcast_to(seg_col, (tok, 128)) == lane, 1.0, 0.0)
-    counts = jnp.sum(onehot, axis=0, keepdims=True)
-    cnt_own[0] = jnp.broadcast_to(counts, (8, 128))
-
-    def count_copy(src, dst, i, peer):
-        c = pltpu.make_async_remote_copy(
-            src_ref=src, dst_ref=dst, send_sem=cnt_ss.at[i], recv_sem=cnt_rs.at[i],
-            device_id={"fsdp": peer}, device_id_type=MESH,
-        )
-        c.start()
-        return c
-
-    cnt = [count_copy(cnt_own.at[0], cnt_recv.at[0], 0, across)]
-    x_cross[2].start()
 
     chosen = frag[0]
 
@@ -223,6 +221,8 @@
     cnt_own[1] = cnt_own[0] + cnt_recv[0]
     for i in range(1, RING):
         cnt.append(count_copy(cnt_own.at[1], cnt_recv.at[i], i, ring[i - 1]))
+    gather_start(1)
+    x_cross[2].start()
     for c in x_loads:
         c.wait()
     lax.fori_loop(0, tok // 16, mean_square, 0)

time: 117 us -> 117 us (level)
  no operation moved by 1% of the time
where the time goes in v5:
time: 117 us; the launch traced here: 116 us
  Pallas kernels  115 us (98%)
  between operations  1.32 us (1%)
    pallas_call x1, Pallas kernels, local(): pl.pallas_call(kernel, out_shape=[pltpu.VMEM((tok, kv), BF16), pltpu.VMEM...  113 us
    pallas_call x1, Pallas kernels, local(): pl.pallas_call(finish, out_shape=[jax.ShapeDtypeStruct((tok, kv), BF16),...  2.42 us

profile of v5, /device:TPU:8, one launch (start us, length us, event | category | flops | bytes accessed | tf_op | source)
XLA Modules:
  0.0 116.4 jit_solution(12875753973898428108)
XLA Ops:
  1.3 0.0 copy-start
  1.3 0.0 copy-start.1
  1.3 112.7 %key_projection.1 = (bf16[320,1024]{1,0:T(8,128)(2,1)S(1)}, bf16[320,5120]{1,0:T(8,128)(2,1)S(1)}, bf16[320,1024]{1,0:T(8,128)(2,1)S(1)}, f32[1,320]{1,0:T(1,128)S(1)}, f32[320,256]{1,0:T(8,128)S(1)}) custom-call(bf16[320,5120]{1,0:T(8,128)(2,1)} %bitcast.6, bf16[320,1024]{1,0:T(8,128)(2,1)} %bitcast.8, s32[1,320]{1,0:T(1,128)} %seg_in.1, f32[1,16]{1,0:T(1,128)} %adv_in.1, ...), custom_call_target="tpu_custom_call" | custom-call | flops 100663296000 | bytes 209715200 | tf_op jit(solution)/shard_map/key_projection/pallas_call | solution.py:546
  114.0 0.0 copy-done
  114.0 0.0 copy-done.1
  114.0 2.4 %finish.1 = (bf16[320,1024]{1,0:T(8,128)(2,1)}, bf16[320,5120]{1,0:T(8,128)(2,1)}, bf16[320,1024]{1,0:T(8,128)(2,1)}, f32[1,320]{1,0:T(1,128)}, f32[320,256]{1,0:T(8,128)}, /*index=5*/f32[320,256]{1,0:T(8,128)}) custom-call(bf16[320,1024]{1,0:T(8,128)(2,1)S(1)} %get-tuple-element.17.keys, bf16[320,5120]{1,0:T(8,128)(2,1)S(1)} %get-tuple-element.18.ig, ...), custom_call_target="tpu_custom_call" | custom-call | tf_op jit(solution)/shard_map/finish/pallas_call | solution.py:566
Async XLA Ops:
  1.3 112.7 %copy-start = (f32[320,1024]{1,0:T(8,128)S(1)}, f32[320,1024]{1,0:T(8,128)}, u32[]{:S(2)}) copy-start(f32[320,1024]{1,0:T(8,128)} %outer.1) | copy-start | bytes 3932164
  1.3 112.7 %copy-start.1 = (f32[320,1024]{1,0:T(8,128)S(1)}, f32[320,1024]{1,0:T(8,128)}, u32[]{:S(2)}) copy-start(f32[320,1024]{1,0:T(8,128)} %moment.1) | copy-start | bytes 3932164
